TPU v7x, 128 devices: a whole 4x4x4 slice. The times are simulated.
128 devices in a mesh: pb: 4 (over x), db: 32 (over z, y, core).
Axes of the slice: x: 4, y: 4, z: 4, core: 2. Of those that a mesh axis runs over, the one named last changes fastest.
Arguments:
- database: bfloat16 [8192, 768], P('db')
- neighbours: int32 [8192, 16], P('db'), may hold values from 0 to 8191, as said below
- valid_count: int32 [8192], P('db'), may hold values from 9 to 16, as said below
- queries: bfloat16 [65536, 768], P('pb'), may hold values from -6 to 6
Outputs:
- augmented: bfloat16 [8192, 768], P('db')
- best_score: float32 [65536], P('pb')
Inputs may be any that keep to these rules, and one draw needn't show every extreme that they name: `neighbours`: every entry is a row number of the whole database, also in slots at or past valid_count (those carry no weight). The owner of row r is r // 256. In each aligned block of 64 rows, at most 64 of its 1024 entries name rows of one owner, and in every block some owner is named by exactly 64 entries. `valid_count`: every aligned block of 64 rows holds a row with 16 valid slots.
All inputs are finite; a program needn't handle non-finite values.
Results may differ from a plain program's by a relative error of at most 0.0028.
Values may be sent and summed in bfloat16 or wider, within the bound.
A program may use at most 128 MiB of HBM per device.

v0:
```python
import functools

import jax
import jax.numpy as jnp
from jax import lax
from jax.experimental import pallas as pl
from jax.experimental.pallas import tpu as pltpu
from jax.sharding import PartitionSpec as P

epsilon = 1e-06
MESH = pl.DeviceIdType.MESH
SIDE = 4
CORES = 2
CHIPS = SIDE * SIDE
SLOTS = (
    (0, 0), (0, 1), (0, 3), (1, 0), (3, 0), (0, 2), (2, 0), (1, 1),
    (1, 3), (3, 1), (3, 3), (1, 2), (2, 1), (3, 2), (2, 3), (2, 2),
)
SLOT_AT = {offset: place for place, offset in enumerate(SLOTS)}
RING = (1, 3, 2)


def inverse_norm(values):
    return lax.rsqrt(jnp.sum(values * values, axis=-1, keepdims=True) + epsilon)


def dot_rows(left, right):
    return lax.dot_general(
        left, right, (((1,), (1,)), ((), ())), preferred_element_type=jnp.float32
    )


def kernel(
    db_ref, nb_ref, vc_ref, q_ref, aug_ref, best_ref,
    q_v, pool, mask_ref, wanted, total, part_in, everyone, tops, rivals, bases,
    q_sem, a_send, a_recv, b_send, b_recv, c_send, c_recv, p_send, p_recv,
    g_send, g_recv, s_send, s_recv, m_send, m_recv, f_send, f_recv, e_send, e_recv,
):
    rows_dev, features = db_ref.shape
    fanout = nb_ref.shape[1]
    own_rows = rows_dev // SIDE
    half = own_rows // 2
    slot_rows = CORES * own_rows
    x = lax.axis_index("pb")
    d = lax.axis_index("db")
    c = d % CORES
    chip = d // CORES
    y = chip % SIDE
    z = chip // SIDE
    mine = pl.multiple_of(x * own_rows, own_rows)

    def plane(dz, dy):
        return (x, ((z + dz) % SIDE * SIDE + (y + dy) % SIDE) * CORES + c)

    sibling = (x, chip * CORES + (1 - c))

    def across(dx):
        return ((x + dx) % SIDE, d)

    def remote(src, dst, send, recv, to):
        return pltpu.make_async_remote_copy(
            src_ref=src, dst_ref=dst, send_sem=send, recv_sem=recv, device_id=to,
            device_id_type=MESH,
        )

    barrier = pltpu.get_barrier_semaphore()
    partners = [plane(dz, dy) for dz, dy in SLOTS[1:]]
    partners += [sibling] + [across(dx) for dx in RING]
    for partner in partners:
        pl.semaphore_signal(barrier, inc=1, device_id=partner, device_id_type=MESH)

    queries_here = q_v.shape[0]
    piece = queries_here // 4
    for k in range(4):
        pltpu.make_async_copy(
            q_ref.at[pl.ds(pl.multiple_of(c * queries_here + k * piece, piece), piece)],
            q_v.at[pl.ds(k * piece, piece)],
            q_sem.at[k],
        ).start()

    pool[pl.ds(0, own_rows), :] = db_ref[pl.ds(mine, own_rows), :]
    pl.semaphore_wait(barrier, len(partners))

    def block(place, core, start, rows):
        return pool.at[pl.ds(place * slot_rows + core * own_rows + start, rows)]

    def copy_a(dz, dy):
        src = SLOT_AT[(0, dy if dz else 0)]
        dst = SLOT_AT[(dz, dy)]
        to = plane(dz, 0) if dz else plane(0, dy)
        return remote(
            block(src, 0, 0, half), block(dst, 0, 0, half), a_send.at[dst], a_recv.at[dst], to
        )

    def copy_b(dz, dy):
        src = SLOT_AT[(dz if dy else 0, 0)]
        dst = SLOT_AT[(dz, dy)]
        to = plane(0, dy) if dy else plane(dz, 0)
        return remote(
            block(src, 0, half, half), block(dst, 0, half, half), b_send.at[dst],
            b_recv.at[dst], to,
        )

    def copy_c(place):
        return remote(
            block(place, 0, 0, own_rows), block(place, 1, 0, own_rows), c_send.at[place],
            c_recv.at[place], sibling,
        )

    def arrival(place, start, sems, recvs):
        spot = block(place, 0, start, half)
        return remote(spot, spot, sems.at[place], recvs.at[place], sibling)

    for step in RING:
        copy_a(0, step).start()
        copy_b(step, 0).start()
    copy_c(0).start()
    for step in RING:
        copy_a(step, 0).start()
        copy_b(0, step).start()

    eye = (
        lax.broadcasted_iota(jnp.int32, (fanout, fanout), 0)
        == lax.broadcasted_iota(jnp.int32, (fanout, fanout), 1)
    ).astype(jnp.float32).astype(jnp.bfloat16)
    ids = nb_ref[...]
    high = dot_rows(eye, (ids // 64).astype(jnp.float32).astype(jnp.bfloat16))
    low = dot_rows(eye, (ids % 64).astype(jnp.float32).astype(jnp.bfloat16))
    place_of = lax.broadcasted_iota(jnp.int32, (fanout, rows_dev), 0)
    wanted[...] = jnp.where(place_of < vc_ref[...], high * 64.0 + low, -1.0)
    for place, (dz, dy) in enumerate(SLOTS):
        for core in range(CORES):
            owner = ((z - dz) % SIDE * SIDE + (y - dy) % SIDE) * CORES + (c + core) % CORES
            bases[place * CORES + core] = owner * rows_dev + x * own_rows

    def build_mask(g, _):
        for u in range(2):
            counts = []
            for core in range(CORES):
                base = bases[(g * 2 + u) * CORES + core]
                number = base + lax.broadcasted_iota(jnp.int32, (own_rows, rows_dev), 0)
                number = number.astype(jnp.float32)
                count = jnp.zeros((own_rows, rows_dev), jnp.float32)
                for k in range(fanout):
                    count = count + jnp.where(wanted[pl.ds(k, 1), :] == number, 1.0, 0.0)
                counts.append(count)
            both = jnp.concatenate(counts, axis=0)
            mask_ref[g, :, pl.ds(u * slot_rows, slot_rows)] = both.T.astype(jnp.bfloat16)
        return 0

    groups = len(SLOTS) // 2
    lax.fori_loop(0, 2, build_mask, 0)

    for step in RING:
        copy_a(0, step).wait_recv()
        for far in RING:
            copy_a(far, step).start()
        copy_b(step, 0).wait_recv()
        for far in RING:
            copy_b(step, far).start()

    lax.fori_loop(2, groups, build_mask, 0)

    for step in RING:
        copy_b(0, step).wait_recv()
        copy_c(SLOT_AT[(0, step)]).start()
        copy_a(step, 0).wait_recv()
        copy_c(SLOT_AT[(step, 0)]).start()
    arrival(7, 0, a_send, a_recv).wait_recv()
    arrival(7, half, b_send, b_recv).wait_recv()
    copy_c(7).start()

    total[...] = jnp.zeros_like(total)
    own = db_ref[...]
    own_inverse = inverse_norm(own.astype(jnp.float32))
    span = 2 * slot_rows

    def take(g, _):
        place = groups + g
        arrival(place, 0, a_send, a_recv).wait_recv()
        arrival(place, half, b_send, b_recv).wait_recv()
        copy_c(place).start()
        copy_c(2 * g).wait_recv()
        copy_c(2 * g + 1).wait_recv()
        rows = pool[pl.ds(pl.multiple_of(g * span, span), span), :]
        squares = rows.astype(jnp.float32)
        squares = squares * squares
        folded = squares[:, 0:128]
        for k in range(1, features // 128):
            folded = folded + squares[:, k * 128 : (k + 1) * 128]
        far_inverse = lax.rsqrt(jnp.sum(folded.T, axis=0, keepdims=True) + epsilon)
        cosine = dot_rows(own, rows) * own_inverse * far_inverse
        halfway = (1.0 + cosine) * 0.5
        weight = halfway * halfway * halfway
        coefficient = (weight * far_inverse).astype(jnp.bfloat16).astype(jnp.float32)
        count = mask_ref[g].astype(jnp.float32)
        spread = jnp.where(count > 0.0, count * coefficient, 0.0)
        spread_high = spread.astype(jnp.bfloat16)
        spread_low = (spread - spread_high.astype(jnp.float32)).astype(jnp.bfloat16)
        total[...] += jnp.dot(spread_high, rows, preferred_element_type=jnp.float32) + jnp.dot(
            spread_low, rows, preferred_element_type=jnp.float32
        )
        return 0

    lax.fori_loop(0, groups, take, 0)

    def quarter(dx):
        return pl.ds(pl.multiple_of((x + dx) % SIDE * own_rows, own_rows), own_rows)

    def copy_p(dx):
        return remote(
            total.at[quarter(dx)], part_in.at[dx - 1], p_send.at[dx], p_recv.at[dx], across(dx)
        )

    for dx in RING:
        copy_p(dx).start()
    kept = db_ref[pl.ds(mine, own_rows), :].astype(jnp.float32)
    summed = kept * inverse_norm(kept) + total[pl.ds(mine, own_rows), :]
    for dx in RING:
        copy_p(dx).wait_recv()
        summed = summed + part_in[dx - 1]
    everyone[pl.ds(mine, own_rows), :] = (summed * inverse_norm(summed)).astype(jnp.bfloat16)

    def copy_g(dx):
        spot = everyone.at[pl.ds(mine, own_rows)]
        return remote(spot, spot, g_send.at[dx], g_recv.at[dx], across(dx))

    def copy_s(dx):
        return remote(
            everyone.at[quarter(-dx)],
            everyone.at[pl.ds(pl.multiple_of(rows_dev + (x - dx) % SIDE * own_rows, own_rows), own_rows)],
            s_send.at[dx], s_recv.at[dx], sibling,
        )

    for dx in RING:
        copy_g(dx).start()
    copy_s(0).start()
    for dx in RING:
        copy_g(dx).wait_recv()
        copy_s(dx).start()
    for dx in range(SIDE):
        copy_s(dx).wait_recv()

    for k in range(4):
        pltpu.make_async_copy(
            q_ref.at[pl.ds(pl.multiple_of(c * queries_here + k * piece, piece), piece)],
            q_v.at[pl.ds(k * piece, piece)],
            q_sem.at[k],
        ).wait()

    share = queries_here // CHIPS
    lines = share // 128

    def chip_at(k):
        return (x, (chip + k) % CHIPS * CORES + c)

    def copy_m(k):
        return remote(tops.at[k], rivals.at[k], m_send.at[k], m_recv.at[k], chip_at(k))

    unroll = 4

    def score(i, _):
        for u in range(unroll):
            k = (i * unroll + u + 1) % CHIPS
            owner = (chip + k) % CHIPS
            panel = q_v[pl.ds(pl.multiple_of(owner * share, share), share), :]
            top = jnp.max(dot_rows(everyone[...], panel), axis=0, keepdims=True)
            for line in range(lines):
                tops[k, pl.ds(line, 1), :] = top[:, line * 128 : (line + 1) * 128]
            if u < unroll - 1:
                copy_m(k).start()
            else:
                @pl.when(i < CHIPS // unroll - 1)
                def _():
                    copy_m(k).start()
        return 0

    lax.fori_loop(0, CHIPS // unroll, score, 0)
    aug_ref[...] = everyone[pl.ds(0, rows_dev), :]
    best = tops[0]
    for k in range(1, CHIPS):
        copy_m(k).wait_recv()
        best = jnp.maximum(best, rivals[k])
    spot = c * CHIPS + chip
    best_ref[spot] = best

    def copy_f(k):
        return remote(
            best_ref.at[spot], best_ref.at[spot], f_send.at[k], f_recv.at[k], chip_at(k)
        )

    for k in range(1, CHIPS):
        copy_f(k).start()
    for k in range(1, CHIPS):
        copy_f(k).wait_recv()
    side = best_ref.at[pl.ds(c * CHIPS, CHIPS)]
    copy_e = remote(side, side, e_send, e_recv, sibling)
    copy_e.start()

    for place in range(1, CHIPS):
        arrival(place, 0, a_send, a_recv).wait_send()
        arrival(place, half, b_send, b_recv).wait_send()
    for place in range(CHIPS):
        copy_c(place).wait_send()
    for dx in RING:
        copy_p(dx).wait_send()
        copy_g(dx).wait_send()
    for dx in range(SIDE):
        copy_s(dx).wait_send()
    for k in range(1, CHIPS):
        copy_m(k).wait_send()
        copy_f(k).wait_send()
    copy_e.wait()


def local(database, neighbours, valid_count, queries):
    rows_dev, features = database.shape
    queries_here = queries.shape[0] // CORES
    own_rows = rows_dev // SIDE
    pool_rows = rows_dev * CHIPS * CORES // SIDE
    share = queries_here // CHIPS
    vmem = pl.BlockSpec(memory_space=pltpu.VMEM)
    dma = pltpu.SemaphoreType.DMA
    augmented, best = pl.pallas_call(
        kernel,
        out_shape=(
            jax.ShapeDtypeStruct((rows_dev, features), jnp.bfloat16),
            jax.ShapeDtypeStruct((CORES * CHIPS, share // 128, 128), jnp.float32),
        ),
        in_specs=[vmem, vmem, vmem, pl.BlockSpec(memory_space=pl.ANY)],
        out_specs=(vmem, vmem),
        scratch_shapes=[
            pltpu.VMEM((queries_here, features), jnp.bfloat16),
            pltpu.VMEM((pool_rows, features), jnp.bfloat16),
            pltpu.VMEM((8, rows_dev, pool_rows // 8), jnp.bfloat16),
            pltpu.VMEM((neighbours.shape[1], rows_dev), jnp.float32),
            pltpu.VMEM((rows_dev, features), jnp.float32),
            pltpu.VMEM((SIDE - 1, own_rows, features), jnp.float32),
            pltpu.VMEM((CORES * rows_dev, features), jnp.bfloat16),
            pltpu.VMEM((CHIPS, share // 128, 128), jnp.float32),
            pltpu.VMEM((CHIPS, share // 128, 128), jnp.float32),
            pltpu.SMEM((CHIPS * CORES,), jnp.int32),
            dma((4,)),
        ]
        + [dma((CHIPS,))] * 6
        + [dma((SIDE,))] * 6
        + [dma((CHIPS,))] * 4
        + [dma, dma],
        compiler_params=pltpu.CompilerParams(
            collective_id=0, has_side_effects=True, vmem_limit_bytes=56 * 2**20
        ),
        name="expand_and_score",
    )(database, neighbours, valid_count.reshape(1, rows_dev), queries)
    return augmented, best.reshape(queries.shape[0])


def solution(mesh):
    return jax.shard_map(
        local,
        mesh=mesh,
        in_specs=(P("db", None), P("db", None), P("db"), P("pb", None)),
        out_specs=(P("db", None), P("pb")),
        check_vma=False,
    )
```

profile of v0, /device:TPU:1, one launch (start us, length us, event | category | flops | bytes accessed | tf_op | source)
XLA Modules:
  0.0 72.5 jit_solution(11152846201655455494)
XLA Ops:
  0.6 1.5 %copy.6.nb_ref = s32[256,16]{1,0:T(8,128)} copy(s32[256,16]{0,1:T(8,128)} %param.5) | data formatting | bytes 32768 | tf_op args[1]
  2.1 67.1 %expand_and_score.1 = (bf16[256,768]{1,0:T(8,128)(2,1)}, f32[32,4,128]{2,1,0:T(4,128)}) custom-call(bf16[256,768]{1,0:T(8,128)(2,1)} %db_ref.1, s32[256,16]{1,0:T(8,128)} %copy.6.nb_ref, s32[1,256]{1,0:T(1,128)} %bitcast.3, bf16[16384,768]{1,0:T(8,128)(2,1)} %q_ref.1), custom_call_target="tpu_custom_call" | custom-call | tf_op jit(solution)/shard_map/expand_and_score/pallas_call | solution.py:324
  69.2 1.8 %copy.9 = bf16[256,768]{1,0:T(8,128)(2,1)} copy(bf16[256,768]{1,0:T(8,128)(2,1)} %get-tuple-element.8) | data formatting | bytes 786432
  71.0 1.5 %copy.10 = f32[16384]{0:T(1024)} copy(f32[16384]{0:T(1024)} %bitcast.2) | data formatting | bytes 131072
where the time goes:
time: 72.7 us; the launch traced here: 72.5 us
  Pallas kernels  67.1 us (92%)
  local copies, waits for them, and re-layouts  4.71 us (6%)
    pallas_call x1, Pallas kernels, local(): pl.pallas_call(kernel, out_shape=(jax.ShapeDtypeStruct((rows_dev, feature...  67.1 us
    unnamed x3, local copies, waits for them, and re-layouts  4.71 us

commit v1 on v0

v1 whole, which is shorter than its diff:
```python
import functools

import jax
import jax.numpy as jnp
from jax import lax
from jax.experimental import pallas as pl
from jax.experimental.pallas import tpu as pltpu
from jax.sharding import PartitionSpec as P

epsilon = 1e-06
MESH = pl.DeviceIdType.MESH
SIDE = 4
CORES = 2
CHIPS = SIDE * SIDE
SLOTS = (
    (0, 0), (0, 1), (0, 3), (1, 0), (3, 0), (0, 2), (2, 0), (1, 1),
    (1, 3), (3, 1), (3, 3), (1, 2), (2, 1), (3, 2), (2, 3), (2, 2),
)
SLOT_AT = {offset: place for place, offset in enumerate(SLOTS)}
RING = (1, 3, 2)


def inverse_norm(values):
    return lax.rsqrt(jnp.sum(values * values, axis=-1, keepdims=True) + epsilon)


def dot_rows(left, right):
    return lax.dot_general(
        left, right, (((1,), (1,)), ((), ())), preferred_element_type=jnp.float32
    )


def kernel(
    db_hbm, nb_hbm, vc_hbm, q_ref, aug_ref, best_ref,
    q_v, db_ref, nb_ref, vc_ref, pool, mask_ref, wanted, total, coded, coded_in, ranges, ranges_in, ranges_of,
    everyone, first_top, tops, rivals, bases,
    q_sem, l_sem, a_send, a_recv, b_send, b_recv, c_send, c_recv, p_send, p_recv, r_send, r_recv,
    g_send, g_recv, s_send, s_recv, m_send, m_recv, f_send, f_recv,
):
    rows_dev, features = db_ref.shape
    fanout = nb_ref.shape[0]
    own_rows = rows_dev // SIDE
    half = own_rows // 2
    slot_rows = CORES * own_rows
    x = lax.axis_index("pb")
    d = lax.axis_index("db")
    c = d % CORES
    chip = d // CORES
    y = chip % SIDE
    z = chip // SIDE
    mine = pl.multiple_of(x * own_rows, own_rows)

    def plane(dz, dy):
        return (x, ((z + dz) % SIDE * SIDE + (y + dy) % SIDE) * CORES + c)

    sibling = (x, chip * CORES + (1 - c))

    def across(dx):
        return ((x + dx) % SIDE, d)

    def remote(src, dst, send, recv, to):
        return pltpu.make_async_remote_copy(
            src_ref=src, dst_ref=dst, send_sem=send, recv_sem=recv, device_id=to,
            device_id_type=MESH,
        )

    barrier = pltpu.get_barrier_semaphore()
    partners = [plane(0, step) for step in RING] + [plane(step, 0) for step in RING]
    partners += [sibling] + [across(step) for step in RING]
    for partner in partners:
        pl.semaphore_signal(barrier, inc=1, device_id=partner, device_id_type=MESH)

    loads = [
        pltpu.make_async_copy(
            db_hbm.at[pl.ds(mine, own_rows)], pool.at[pl.ds(0, own_rows)], l_sem.at[0]
        ),
        pltpu.make_async_copy(nb_hbm, nb_ref, l_sem.at[1]),
        pltpu.make_async_copy(vc_hbm, vc_ref, l_sem.at[2]),
        pltpu.make_async_copy(db_hbm, db_ref, l_sem.at[3]),
    ]
    for load in loads:
        load.start()

    queries_here = q_v.shape[0]
    piece = queries_here // 4
    query_loads = [
        pltpu.make_async_copy(
            q_ref.at[pl.ds(pl.multiple_of(c * queries_here + k * piece, piece), piece)],
            q_v.at[pl.ds(k * piece, piece)],
            q_sem.at[k],
        )
        for k in range(4)
    ]
    for load in query_loads:
        load.start()
    for load in loads:
        load.wait()
    pl.semaphore_wait(barrier, len(partners))

    def block(place, core, start, rows):
        return pool.at[pl.ds(place * slot_rows + core * own_rows + start, rows)]

    def copy_a(dz, dy):
        src = SLOT_AT[(0, dy if dz else 0)]
        dst = SLOT_AT[(dz, dy)]
        to = plane(dz, 0) if dz else plane(0, dy)
        return remote(
            block(src, 0, 0, half), block(dst, 0, 0, half), a_send.at[dst], a_recv.at[dst], to
        )

    def copy_b(dz, dy):
        src = SLOT_AT[(dz if dy else 0, 0)]
        dst = SLOT_AT[(dz, dy)]
        to = plane(0, dy) if dy else plane(dz, 0)
        return remote(
            block(src, 0, half, half), block(dst, 0, half, half), b_send.at[dst],
            b_recv.at[dst], to,
        )

    def copy_c(place):
        return remote(
            block(place, 0, 0, own_rows), block(place, 1, 0, own_rows), c_send.at[place],
            c_recv.at[place], sibling,
        )

    def arrival(place, start, sems, recvs):
        spot = block(place, 0, start, half)
        return remote(spot, spot, sems.at[place], recvs.at[place], sibling)

    for step in RING:
        copy_a(0, step).start()
        copy_b(step, 0).start()
    copy_c(0).start()
    for step in RING:
        copy_a(step, 0).start()
        copy_b(0, step).start()

    place_of = lax.broadcasted_iota(jnp.int32, (fanout, rows_dev), 0)
    wanted[...] = jnp.where(place_of < vc_ref[...], nb_ref[...], -1)
    for place, (dz, dy) in enumerate(SLOTS):
        for core in range(CORES):
            owner = ((z - dz) % SIDE * SIDE + (y - dy) % SIDE) * CORES + (c + core) % CORES
            bases[place * CORES + core] = owner * rows_dev + x * own_rows

    def build_mask(g, _):
        for u in range(2):
            counts = []
            for core in range(CORES):
                base = bases[(g * 2 + u) * CORES + core]
                number = base + lax.broadcasted_iota(jnp.int32, (own_rows, rows_dev), 0)
                count = jnp.zeros((own_rows, rows_dev), jnp.float32)
                for k in range(fanout):
                    count = count + jnp.where(wanted[pl.ds(k, 1), :] == number, 1.0, 0.0)
                counts.append(count)
            both = jnp.concatenate(counts, axis=0)
            mask_ref[g, :, pl.ds(u * slot_rows, slot_rows)] = both.T.astype(jnp.bfloat16)
        return 0

    groups = len(SLOTS) // 2
    lax.fori_loop(0, 2, build_mask, 0)

    for step in RING:
        copy_a(0, step).wait_recv()
        for far in RING:
            copy_a(far, step).start()
        copy_b(step, 0).wait_recv()
        for far in RING:
            copy_b(step, far).start()

    lax.fori_loop(2, groups, build_mask, 0)

    for step in RING:
        copy_b(0, step).wait_recv()
        copy_c(SLOT_AT[(0, step)]).start()
        copy_a(step, 0).wait_recv()
        copy_c(SLOT_AT[(step, 0)]).start()

    def pass_on(place):
        arrival(place, 0, a_send, a_recv).wait_recv()
        arrival(place, half, b_send, b_recv).wait_recv()
        copy_c(place).start()

    total[...] = jnp.zeros_like(total)
    own = db_ref[...]
    own_inverse = inverse_norm(own.astype(jnp.float32))
    span = 2 * slot_rows

    def take(g):
        copy_c(2 * g).wait_recv()
        copy_c(2 * g + 1).wait_recv()
        rows = pool[pl.ds(pl.multiple_of(g * span, span), span), :]
        squares = rows.astype(jnp.float32)
        squares = squares * squares
        folded = squares[:, 0:128]
        for k in range(1, features // 128):
            folded = folded + squares[:, k * 128 : (k + 1) * 128]
        far_inverse = lax.rsqrt(jnp.sum(folded.T, axis=0, keepdims=True) + epsilon)
        cosine = dot_rows(own, rows) * own_inverse * far_inverse
        halfway = (1.0 + cosine) * 0.5
        weight = halfway * halfway * halfway
        coefficient = (weight * far_inverse).astype(jnp.bfloat16).astype(jnp.float32)
        count = mask_ref[g].astype(jnp.float32)
        spread = jnp.where(count > 0.0, count * coefficient, 0.0)
        spread_high = spread.astype(jnp.bfloat16)
        spread_low = (spread - spread_high.astype(jnp.float32)).astype(jnp.bfloat16)
        total[...] += jnp.dot(spread_high, rows, preferred_element_type=jnp.float32) + jnp.dot(
            spread_low, rows, preferred_element_type=jnp.float32
        )

    def take_early(g, _):
        take(g)
        return 0

    def take_late(g, _):
        for ahead in (3, 4):
            place = 2 * g + ahead

            @pl.when(place < CHIPS)
            def _():
                pass_on(place)

        take(g)
        return 0

    lax.fori_loop(0, 3, take_early, 0)
    pass_on(7)
    pass_on(8)
    lax.fori_loop(3, groups, take_late, 0)

    partial = total[...]
    largest = jnp.max(jnp.abs(partial), axis=-1, keepdims=True)
    largest = jnp.maximum(largest, 1e-30)
    coded[...] = jnp.round(partial * (32760.0 / largest)).astype(jnp.int32).astype(jnp.int16)
    spread_range = jnp.broadcast_to(largest * (1.0 / 32760.0), (rows_dev, 128))
    ranges[...] = spread_range.T[0:8, :]

    def quarter(dx, h):
        start = (x + dx) % SIDE * own_rows + h * half
        return pl.ds(pl.multiple_of(start, half), half)

    def copy_r(dx):
        return remote(ranges, ranges_in.at[dx - 1], r_send.at[dx], r_recv.at[dx], across(dx))

    def copy_p(dx, h):
        at = h * SIDE + dx
        return remote(
            coded.at[quarter(dx, h)], coded_in.at[dx - 1, pl.ds(h * half, half)],
            p_send.at[at], p_recv.at[at], across(dx),
        )

    for dx in RING:
        copy_r(dx).start()
    for h in range(2):
        for dx in RING:
            copy_p(dx, h).start()

    def spot(h, core, chip_x):
        start = (h * CORES + core) * SIDE * half + chip_x * half
        return pl.ds(pl.multiple_of(start, half), half)

    def copy_g(dx, h):
        at = h * SIDE + dx
        here = everyone.at[spot(h, 0, x)]
        return remote(here, here, g_send.at[at], g_recv.at[at], across(dx))

    def copy_s(dx, h):
        at = h * SIDE + dx
        from_x = (x + SIDE - dx) % SIDE
        return remote(
            everyone.at[spot(h, 0, from_x)], everyone.at[spot(h, 1, from_x)], s_send.at[at],
            s_recv.at[at], sibling,
        )

    sums = []
    for h in range(2):
        kept = db_ref[quarter(0, h), :].astype(jnp.float32)
        sums.append(kept * inverse_norm(kept) + total[quarter(0, h), :])
    for dx in RING:
        copy_r(dx).wait_recv()
        across_range = jnp.broadcast_to(ranges_in[dx - 1, 0:1, :], (128, rows_dev))
        ranges_of[dx - 1] = across_range.T

    for h in range(2):
        summed = sums[h]
        for dx in RING:
            copy_p(dx, h).wait_recv()
            part = coded_in[dx - 1, pl.ds(h * half, half), :].astype(jnp.float32)
            summed = summed + part * ranges_of[dx - 1, quarter(0, h), 0:1]
        everyone[spot(h, 0, x), :] = (summed * inverse_norm(summed)).astype(jnp.bfloat16)
        for dx in RING:
            copy_g(dx, h).start()
        copy_s(0, h).start()

    def hand_over(h):
        for dx in RING:
            copy_g(dx, h).wait_recv()
            copy_s(dx, h).start()

    hand_over(0)
    for load in query_loads:
        load.wait()
    for dx in range(SIDE):
        copy_s(dx, 0).wait_recv()

    share = queries_here // CHIPS
    lines = share // 128
    part_rows = CORES * SIDE * half

    def chip_at(k):
        return (x, (chip + k) % CHIPS * CORES + c)

    def copy_m(k):
        return remote(tops.at[k], rivals.at[k], m_send.at[k], m_recv.at[k], chip_at(k))

    def folded_scores(h, k):
        owner = (chip + k) % CHIPS
        panel = q_v[pl.ds(pl.multiple_of(owner * share, share), share), :]
        scores = dot_rows(everyone[pl.ds(h * part_rows, part_rows), :], panel)
        return jnp.max(scores.reshape(part_rows // 8, 8, share), axis=0)

    unroll = 4

    def score_first(i, _):
        for u in range(unroll):
            k = (i * unroll + u + 1) % CHIPS
            first_top[k] = folded_scores(0, k)
        return 0

    def score_second(i, _):
        for u in range(unroll):
            k = (i * unroll + u + 1) % CHIPS
            top = jnp.maximum(first_top[k], folded_scores(1, k))
            top = jnp.max(top, axis=0, keepdims=True)
            for line in range(lines):
                tops[k, pl.ds(line, 1), :] = top[:, line * 128 : (line + 1) * 128]
            if u < unroll - 1:
                copy_m(k).start()
            else:
                @pl.when(i < CHIPS // unroll - 1)
                def _():
                    copy_m(k).start()
        return 0

    lax.fori_loop(0, 1, score_first, 0)
    hand_over(1)
    lax.fori_loop(1, CHIPS // unroll, score_first, 0)
    for dx in range(SIDE):
        copy_s(dx, 1).wait_recv()
    lax.fori_loop(0, CHIPS // unroll, score_second, 0)

    for chip_x in range(SIDE):
        for h in range(2):
            start = h * part_rows + chip_x * half
            aug_ref[pl.ds(chip_x * own_rows + h * half, half), :] = everyone[pl.ds(start, half), :]
    best = tops[0]
    for k in range(1, CHIPS):
        copy_m(k).wait_recv()
        best = jnp.maximum(best, rivals[k])
    here = c * CHIPS + chip
    best_ref[here] = best
    devices = CHIPS * CORES

    def copy_f(k):
        return remote(
            best_ref.at[here], best_ref.at[here], f_send.at[k], f_recv.at[k],
            (x, (d + k) % devices),
        )

    for k in range(1, devices):
        copy_f(k).start()

    for place in range(1, CHIPS):
        arrival(place, 0, a_send, a_recv).wait_send()
        arrival(place, half, b_send, b_recv).wait_send()
    for place in range(CHIPS):
        copy_c(place).wait_send()
    for dx in RING:
        copy_r(dx).wait_send()
    for h in range(2):
        for dx in RING:
            copy_p(dx, h).wait_send()
            copy_g(dx, h).wait_send()
        for dx in range(SIDE):
            copy_s(dx, h).wait_send()
    for k in range(1, CHIPS):
        copy_m(k).wait_send()
    for k in range(1, devices):
        copy_f(k).wait()


def local(database, neighbours, valid_count, queries):
    rows_dev, features = database.shape
    fanout = neighbours.shape[1]
    queries_here = queries.shape[0] // CORES
    own_rows = rows_dev // SIDE
    pool_rows = rows_dev * CHIPS * CORES // SIDE
    share = queries_here // CHIPS
    vmem = pl.BlockSpec(memory_space=pltpu.VMEM)
    anywhere = pl.BlockSpec(memory_space=pl.ANY)
    dma = pltpu.SemaphoreType.DMA
    augmented, best = pl.pallas_call(
        kernel,
        out_shape=(
            jax.ShapeDtypeStruct((rows_dev, features), jnp.bfloat16),
            jax.ShapeDtypeStruct((CORES * CHIPS, share // 128, 128), jnp.float32),
        ),
        in_specs=[anywhere, anywhere, anywhere, anywhere],
        out_specs=(vmem, vmem),
        scratch_shapes=[
            pltpu.VMEM((queries_here, features), jnp.bfloat16),
            pltpu.VMEM((rows_dev, features), jnp.bfloat16),
            pltpu.VMEM((fanout, rows_dev), jnp.int32),
            pltpu.VMEM((1, rows_dev), jnp.int32),
            pltpu.VMEM((pool_rows, features), jnp.bfloat16),
            pltpu.VMEM((8, rows_dev, pool_rows // 8), jnp.bfloat16),
            pltpu.VMEM((fanout, rows_dev), jnp.int32),
            pltpu.VMEM((rows_dev, features), jnp.float32),
            pltpu.VMEM((rows_dev, features), jnp.int16),
            pltpu.VMEM((SIDE - 1, own_rows, features), jnp.int16),
            pltpu.VMEM((8, rows_dev), jnp.float32),
            pltpu.VMEM((SIDE - 1, 8, rows_dev), jnp.float32),
            pltpu.VMEM((SIDE - 1, rows_dev, 128), jnp.float32),
            pltpu.VMEM((CORES * rows_dev, features), jnp.bfloat16),
            pltpu.VMEM((CHIPS, 8, share), jnp.float32),
            pltpu.VMEM((CHIPS, share // 128, 128), jnp.float32),
            pltpu.VMEM((CHIPS, share // 128, 128), jnp.float32),
            pltpu.SMEM((CHIPS * CORES,), jnp.int32),
            dma((4,)),
            dma((4,)),
        ]
        + [dma((CHIPS,))] * 6
        + [dma((2 * SIDE,))] * 2
        + [dma((SIDE,))] * 2
        + [dma((2 * SIDE,))] * 4
        + [dma((CHIPS,))] * 2
        + [dma((CHIPS * CORES,))] * 2,
        compiler_params=pltpu.CompilerParams(
            collective_id=0, has_side_effects=True, vmem_limit_bytes=56 * 2**20
        ),
        name="expand_and_score",
    )(database, neighbours.T, valid_count.reshape(1, rows_dev), queries)
    return augmented, best.reshape(queries.shape[0])


def solution(mesh):
    return jax.shard_map(
        local,
        mesh=mesh,
        in_specs=(P("db", None), P("db", None), P("db"), P("pb", None)),
        out_specs=(P("db", None), P("pb")),
        check_vma=False,
    )
```

time: 72.7 us -> 64.7 us (0.89)
  Pallas kernels: 67.1 us -> 60.6 us
  local copies, waits for them, and re-layouts: 4.71 us -> 3.24 us
    pallas_call x1, Pallas kernels: 67.1 us -> 60.6 us  [local(): pl.pallas_call(kernel, out_shape=(jax.ShapeDtypeStruct((rows_dev, feature...]
    unnamed x3 -> x2, local copies, waits for them, and re-layouts: 4.71 us -> 3.24 us
where the time goes in v1:
time: 64.7 us; the launch traced here: 64.5 us
  Pallas kernels  60.6 us (94%)
  local copies, waits for them, and re-layouts  3.24 us (5%)
    pallas_call x1, Pallas kernels, local(): pl.pallas_call(kernel, out_shape=(jax.ShapeDtypeStruct((rows_dev, feature...  60.6 us
    unnamed x2, local copies, waits for them, and re-layouts  3.24 us

profile of v1, /device:TPU:1, one launch (start us, length us, event | category | flops | bytes accessed | tf_op | source)
XLA Modules:
  0.0 64.5 jit_solution(15858766127425485393)
XLA Ops:
  0.6 60.6 %expand_and_score.1 = (bf16[256,768]{1,0:T(8,128)(2,1)}, f32[32,4,128]{2,1,0:T(4,128)}) custom-call(bf16[256,768]{1,0:T(8,128)(2,1)} %db_hbm.1, s32[16,256]{1,0:T(8,128)} %bitcast.4, s32[1,256]{1,0:T(1,128)} %bitcast.5, bf16[16384,768]{1,0:T(8,128)(2,1)} %q_ref.1), custom_call_target="tpu_custom_call" | custom-call | tf_op jit(solution)/shard_map/expand_and_score/pallas_call | solution.py:401
  61.3 1.8 %copy.8 = bf16[256,768]{1,0:T(8,128)(2,1)} copy(bf16[256,768]{1,0:T(8,128)(2,1)} %get-tuple-element.8) | data formatting | bytes 786432
  63.1 1.5 %copy.9 = f32[16384]{0:T(1024)} copy(f32[16384]{0:T(1024)} %bitcast.3) | data formatting | bytes 131072

commit v2 on v1

v2 whole, which is shorter than its diff:
```python
import functools

import jax
import jax.numpy as jnp
from jax import lax
from jax.experimental import pallas as pl
from jax.experimental.pallas import tpu as pltpu
from jax.sharding import PartitionSpec as P

epsilon = 1e-06
MESH = pl.DeviceIdType.MESH
SIDE = 4
CORES = 2
CHIPS = SIDE * SIDE
SLOTS = (
    (0, 0), (0, 1), (0, 3), (1, 0), (3, 0), (0, 2), (2, 0), (1, 1),
    (1, 3), (3, 1), (3, 3), (1, 2), (2, 1), (3, 2), (2, 3), (2, 2),
)
SLOT_AT = {offset: place for place, offset in enumerate(SLOTS)}
RING = (1, 3, 2)


def inverse_norm(values):
    return lax.rsqrt(jnp.sum(values * values, axis=-1, keepdims=True) + epsilon)


def dot_rows(left, right):
    return lax.dot_general(
        left, right, (((1,), (1,)), ((), ())), preferred_element_type=jnp.float32
    )


def kernel(
    db_hbm, nb_hbm, vc_hbm, q_ref, aug_ref, best_ref,
    q_v, db_ref, nb_ref, vc_ref, pool, mask_ref, wanted, total, coded, coded_in, ranges, ranges_in, ranges_of,
    everyone, first_top, tops, rivals, bases,
    q_sem, l_sem, a_recv, b_recv, c_recv, p_recv, g_recv, s_recv, ab_send, c_send, r_send, r_recv,
    p_send, g_send, s_send, m_send, m_recv, f_send, f_recv,
):
    rows_dev, features = db_ref.shape
    fanout = nb_ref.shape[0]
    own_rows = rows_dev // SIDE
    half = own_rows // 2
    parity_rows = CHIPS * own_rows
    span = 4 * own_rows
    x = lax.axis_index("pb")
    d = lax.axis_index("db")
    c = d % CORES
    chip = d // CORES
    y = chip % SIDE
    z = chip // SIDE
    mine = pl.multiple_of(x * own_rows, own_rows)

    def plane(dz, dy):
        return (x, ((z + dz) % SIDE * SIDE + (y + dy) % SIDE) * CORES + c)

    sibling = (x, chip * CORES + (1 - c))

    def across(dx):
        return ((x + dx) % SIDE, d)

    def remote(src, dst, send, recv, to):
        return pltpu.make_async_remote_copy(
            src_ref=src, dst_ref=dst, send_sem=send, recv_sem=recv, device_id=to,
            device_id_type=MESH,
        )

    loads = [
        pltpu.make_async_copy(
            db_hbm.at[pl.ds(mine, own_rows)], pool.at[pl.ds(0, own_rows)], l_sem.at[0]
        ),
        pltpu.make_async_copy(nb_hbm, nb_ref, l_sem.at[1]),
        pltpu.make_async_copy(vc_hbm, vc_ref, l_sem.at[2]),
        pltpu.make_async_copy(db_hbm, db_ref, l_sem.at[3]),
    ]
    loads[0].start()

    barrier = pltpu.get_barrier_semaphore()
    partners = [plane(0, step) for step in RING] + [plane(step, 0) for step in RING]
    partners += [sibling] + [across(step) for step in RING]
    for partner in partners:
        pl.semaphore_signal(barrier, inc=1, device_id=partner, device_id_type=MESH)

    for load in loads[1:]:
        load.start()

    loads[0].wait()
    pl.semaphore_wait(barrier, len(partners))

    def block(place, core, start, rows):
        return pool.at[pl.ds(core * parity_rows + place * own_rows + start, rows)]

    def copy_a(dz, dy):
        src = SLOT_AT[(0, dy if dz else 0)]
        dst = SLOT_AT[(dz, dy)]
        to = plane(dz, 0) if dz else plane(0, dy)
        return remote(
            block(src, 0, 0, half), block(dst, 0, 0, half), ab_send, a_recv.at[dst], to
        )

    def copy_b(dz, dy):
        src = SLOT_AT[(dz if dy else 0, 0)]
        dst = SLOT_AT[(dz, dy)]
        to = plane(0, dy) if dy else plane(dz, 0)
        return remote(
            block(src, 0, half, half), block(dst, 0, half, half), ab_send,
            (a_recv if dz and dy else b_recv).at[dst], to,
        )

    def copy_c(place):
        return remote(
            block(place, 0, 0, own_rows), block(place, 1, 0, own_rows), c_send,
            c_recv.at[place // 4], sibling,
        )

    for step in RING:
        copy_a(0, step).start()
        copy_b(step, 0).start()
    copy_c(0).start()
    for step in RING:
        copy_a(step, 0).start()
        copy_b(0, step).start()

    queries_here = q_v.shape[0]
    piece = queries_here // 4
    query_loads = [
        pltpu.make_async_copy(
            q_ref.at[pl.ds(pl.multiple_of(c * queries_here + k * piece, piece), piece)],
            q_v.at[pl.ds(k * piece, piece)],
            q_sem.at[k],
        )
        for k in range(4)
    ]
    for load in query_loads:
        load.start()
    for load in loads[1:]:
        load.wait()

    place_of = lax.broadcasted_iota(jnp.int32, (fanout, rows_dev), 0)
    wanted[...] = jnp.where(place_of < vc_ref[...], nb_ref[...], -1)
    for place, (dz, dy) in enumerate(SLOTS):
        for core in range(CORES):
            owner = ((z - dz) % SIDE * SIDE + (y - dy) % SIDE) * CORES + (c + core) % CORES
            bases[core * CHIPS + place] = owner * rows_dev + x * own_rows

    def build_mask(part):
        for u in range(2):
            counts = []
            for v in range(2):
                base = bases[part * 4 + u * 2 + v]
                number = base + lax.broadcasted_iota(jnp.int32, (own_rows, rows_dev), 0)
                count = jnp.zeros((own_rows, rows_dev), jnp.float32)
                for k in range(fanout):
                    count = count + jnp.where(wanted[pl.ds(k, 1), :] == number, 1.0, 0.0)
                counts.append(count)
            both = jnp.concatenate(counts, axis=0)
            mask_ref[part, :, pl.ds(u * 2 * own_rows, 2 * own_rows)] = both.T.astype(jnp.bfloat16)

    def first_masks(i, _):
        build_mask(4 * i)
        return 0

    def other_masks(i, _):
        build_mask(i + 1 + i // 3)
        return 0

    lax.fori_loop(0, 2, first_masks, 0)

    for step in RING:
        copy_a(0, step).wait_recv()
        for far in RING:
            copy_a(far, step).start()
        copy_b(step, 0).wait_recv()
        for far in RING:
            copy_b(step, far).start()

    lax.fori_loop(0, 6, other_masks, 0)

    for step in RING:
        copy_b(0, step).wait_recv()
        copy_c(SLOT_AT[(0, step)]).start()
        copy_a(step, 0).wait_recv()
        copy_c(SLOT_AT[(step, 0)]).start()

    def pass_on(place):
        here = block(place, 0, 0, own_rows)
        remote(here, here, ab_send, a_recv.at[place], sibling).wait_recv()
        copy_c(place).start()

    total[...] = jnp.zeros_like(total)
    own = db_ref[...]
    own_inverse = inverse_norm(own.astype(jnp.float32))

    def take(g):
        rows = pool[pl.ds(pl.multiple_of(g * span, span), span), :]
        squares = rows.astype(jnp.float32)
        squares = squares * squares
        folded = squares[:, 0:128]
        for k in range(1, features // 128):
            folded = folded + squares[:, k * 128 : (k + 1) * 128]
        far_inverse = lax.rsqrt(jnp.sum(folded.T, axis=0, keepdims=True) + epsilon)
        cosine = dot_rows(own, rows) * own_inverse * far_inverse
        halfway = (1.0 + cosine) * 0.5
        weight = halfway * halfway * halfway
        coefficient = (weight * far_inverse).astype(jnp.bfloat16).astype(jnp.float32)
        count = mask_ref[g].astype(jnp.float32)
        spread = jnp.where(count > 0.0, count * coefficient, 0.0)
        total[...] += jnp.dot(
            spread.astype(jnp.bfloat16), rows, preferred_element_type=jnp.float32
        )

    def step_over(i, _):
        part = jnp.where(i < 4, i // 2 + i % 2 * 4, jnp.where(i < 6, i - 2, i))

        @pl.when(i == 2)
        def _():
            pass_on(7)

        @pl.when((i == 4) | (i == 5))
        def _():
            for u in range(4):
                pass_on(part * 4 + u)

        @pl.when(part >= 4)
        def _():
            here = pool.at[pl.ds(pl.multiple_of(part * span, span), span)]
            remote(here, here, c_send, c_recv.at[part - 4], sibling).wait_recv()

        take(part)
        return 0

    lax.fori_loop(0, 8, step_over, 0)

    partial = total[...]
    largest = jnp.max(jnp.abs(partial), axis=-1, keepdims=True)
    largest = jnp.maximum(largest, 1e-30)
    coded[...] = jnp.round(partial * (32760.0 / largest)).astype(jnp.int32).astype(jnp.int16)
    spread_range = jnp.broadcast_to(largest * (1.0 / 32760.0), (rows_dev, 128))
    ranges[...] = spread_range.T[0:8, :]

    def quarter(dx, h):
        start = (x + dx) % SIDE * own_rows + h * half
        return pl.ds(pl.multiple_of(start, half), half)

    def copy_r(dx):
        return remote(ranges, ranges_in.at[dx - 1], r_send, r_recv, across(dx))

    def copy_p(dx, h):
        return remote(
            coded.at[quarter(dx, h)], coded_in.at[h, dx - 1], p_send, p_recv.at[h], across(dx)
        )

    for dx in RING:
        copy_p(dx, 0).start()
    for dx in RING:
        copy_r(dx).start()
    for dx in RING:
        copy_p(dx, 1).start()

    def spot(h, core, chip_x):
        start = (h * CORES + core) * SIDE * half + chip_x * half
        return pl.ds(pl.multiple_of(start, half), half)

    def copy_g(dx, h):
        at = h * SIDE + dx
        here = everyone.at[spot(h, 0, x)]
        return remote(here, here, g_send, g_recv.at[at], across(dx))

    def copy_s(dx, h):
        from_x = (x + SIDE - dx) % SIDE
        return remote(
            everyone.at[spot(h, 0, from_x)], everyone.at[spot(h, 1, from_x)], s_send,
            s_recv.at[h], sibling,
        )

    def sibling_rows(h):
        start = (h * CORES + 1) * SIDE * half
        here = everyone.at[pl.ds(start, SIDE * half)]
        return remote(here, here, s_send, s_recv.at[h], sibling)

    sums = []
    for h in range(2):
        kept = db_ref[quarter(0, h), :].astype(jnp.float32)
        sums.append(kept * inverse_norm(kept) + total[quarter(0, h), :])
    remote(ranges_in, ranges_in, r_send, r_recv, sibling).wait_recv()
    for dx in RING:
        across_range = jnp.broadcast_to(ranges_in[dx - 1, 0:1, :], (128, rows_dev))
        ranges_of[dx - 1] = across_range.T

    for h in range(2):
        summed = sums[h]
        here = coded_in.at[h]
        remote(here, here, p_send, p_recv.at[h], sibling).wait_recv()
        for dx in RING:
            part = coded_in[h, dx - 1].astype(jnp.float32)
            summed = summed + part * ranges_of[dx - 1, quarter(0, h), 0:1]
        everyone[spot(h, 0, x), :] = (summed * inverse_norm(summed)).astype(jnp.bfloat16)
        for dx in RING:
            copy_g(dx, h).start()
        copy_s(0, h).start()

    def hand_over(h):
        for dx in RING:
            copy_g(dx, h).wait_recv()
            copy_s(dx, h).start()

    hand_over(0)
    for load in query_loads:
        load.wait()
    sibling_rows(0).wait_recv()

    share = queries_here // CHIPS
    lines = share // 128
    part_rows = CORES * SIDE * half

    def chip_at(k):
        return (x, (chip + k) % CHIPS * CORES + c)

    def copy_m(k):
        return remote(tops.at[k], rivals.at[k], m_send, m_recv, chip_at(k))

    def folded_scores(h, k):
        owner = (chip + k) % CHIPS
        panel = q_v[pl.ds(pl.multiple_of(owner * share, share), share), :]
        scores = dot_rows(everyone[pl.ds(h * part_rows, part_rows), :], panel)
        return jnp.max(scores.reshape(part_rows // 8, 8, share), axis=0)

    unroll = 4

    def score_first(i, _):
        for u in range(unroll):
            k = (i * unroll + u + 1) % CHIPS
            first_top[k] = folded_scores(0, k)
        return 0

    def score_second(i, _):
        for u in range(unroll):
            k = (i * unroll + u + 1) % CHIPS
            top = jnp.maximum(first_top[k], folded_scores(1, k))
            top = jnp.max(top, axis=0, keepdims=True)
            for line in range(lines):
                tops[k, pl.ds(line, 1), :] = top[:, line * 128 : (line + 1) * 128]
        for u in range(unroll - 1):
            copy_m(i * unroll + u + 1).start()

        @pl.when(i < CHIPS // unroll - 1)
        def _():
            copy_m((i + 1) * unroll).start()

        return 0

    lax.fori_loop(0, 1, score_first, 0)
    hand_over(1)
    lax.fori_loop(1, CHIPS // unroll, score_first, 0)
    sibling_rows(1).wait_recv()
    lax.fori_loop(0, CHIPS // unroll, score_second, 0)

    for chip_x in range(SIDE):
        for h in range(2):
            start = h * part_rows + chip_x * half
            aug_ref[pl.ds(chip_x * own_rows + h * half, half), :] = everyone[pl.ds(start, half), :]
    others = pl.ds(1, CHIPS - 1)
    remote(tops.at[others], rivals.at[others], m_send, m_recv, sibling).wait_recv()
    best = tops[0]
    for k in range(1, CHIPS):
        best = jnp.maximum(best, rivals[k])
    here = c * CHIPS + chip
    best_ref[here] = best
    devices = CHIPS * CORES

    def copy_f(k):
        return remote(
            best_ref.at[here], best_ref.at[here], f_send, f_recv, (x, (d + k) % devices)
        )

    for k in range(1, devices):
        copy_f(k).start()

    def sent(ref, sem):
        remote(ref, ref, sem, sem, sibling).wait_send()

    sent(pool.at[pl.ds(0, 2 * (CHIPS - 1) * half)], ab_send)
    sent(pool.at[pl.ds(0, parity_rows)], c_send)
    sent(ranges_in, r_send)
    sent(coded_in, p_send)
    sent(everyone.at[pl.ds(0, 6 * half)], g_send)
    sent(everyone.at[pl.ds(0, 8 * half)], s_send)
    sent(tops.at[others], m_send)
    arrived = best_ref.at[pl.ds(0, devices - 1)]
    remote(arrived, arrived, f_send, f_recv, sibling).wait()


def deliver(rows_in, best_in, rows_out, best_out):
    rows_out[...] = rows_in[...]
    best_out[...] = best_in[...]


def local(database, neighbours, valid_count, queries):
    rows_dev, features = database.shape
    fanout = neighbours.shape[1]
    queries_here = queries.shape[0] // CORES
    own_rows = rows_dev // SIDE
    pool_rows = rows_dev * CHIPS * CORES // SIDE
    share = queries_here // CHIPS
    vmem = pl.BlockSpec(memory_space=pltpu.VMEM)
    anywhere = pl.BlockSpec(memory_space=pl.ANY)
    dma = pltpu.SemaphoreType.DMA
    augmented, best = pl.pallas_call(
        kernel,
        out_shape=(
            jax.ShapeDtypeStruct((rows_dev, features), jnp.bfloat16),
            jax.ShapeDtypeStruct((CORES * CHIPS, share // 128, 128), jnp.float32),
        ),
        in_specs=[anywhere, anywhere, anywhere, anywhere],
        out_specs=(vmem, vmem),
        scratch_shapes=[
            pltpu.VMEM((queries_here, features), jnp.bfloat16),
            pltpu.VMEM((rows_dev, features), jnp.bfloat16),
            pltpu.VMEM((fanout, rows_dev), jnp.int32),
            pltpu.VMEM((1, rows_dev), jnp.int32),
            pltpu.VMEM((pool_rows, features), jnp.bfloat16),
            pltpu.VMEM((8, rows_dev, pool_rows // 8), jnp.bfloat16),
            pltpu.VMEM((fanout, rows_dev), jnp.int32),
            pltpu.VMEM((rows_dev, features), jnp.float32),
            pltpu.VMEM((rows_dev, features), jnp.int16),
            pltpu.VMEM((2, SIDE - 1, own_rows // 2, features), jnp.int16),
            pltpu.VMEM((8, rows_dev), jnp.float32),
            pltpu.VMEM((SIDE - 1, 8, rows_dev), jnp.float32),
            pltpu.VMEM((SIDE - 1, rows_dev, 128), jnp.float32),
            pltpu.VMEM((CORES * rows_dev, features), jnp.bfloat16),
            pltpu.VMEM((CHIPS, 8, share), jnp.float32),
            pltpu.VMEM((CHIPS, share // 128, 128), jnp.float32),
            pltpu.VMEM((CHIPS, share // 128, 128), jnp.float32),
            pltpu.SMEM((CHIPS * CORES,), jnp.int32),
            dma((4,)),
            dma((4,)),
        ]
        + [dma((CHIPS,))] * 2
        + [dma((4,)), dma((2,)), dma((2 * SIDE,)), dma((2,))]
        + [dma] * 11,
        compiler_params=pltpu.CompilerParams(
            collective_id=0, has_side_effects=True, vmem_limit_bytes=56 * 2**20
        ),
        name="expand_and_score",
    )(database, neighbours.T, valid_count.reshape(1, rows_dev), queries)
    augmented, best = pl.pallas_call(
        deliver,
        out_shape=(
            jax.ShapeDtypeStruct(augmented.shape, augmented.dtype),
            jax.ShapeDtypeStruct(best.shape, best.dtype),
        ),
        in_specs=[vmem, vmem],
        out_specs=(vmem, vmem),
        name="deliver",
    )(augmented, best)
    return augmented, best.reshape(queries.shape[0])


def solution(mesh):
    return jax.shard_map(
        local,
        mesh=mesh,
        in_specs=(P("db", None), P("db", None), P("db"), P("pb", None)),
        out_specs=(P("db", None), P("pb")),
        check_vma=False,
    )
```

time: 64.7 us -> 56 us (0.87)
  Pallas kernels: 60.6 us -> 55.2 us
  local copies, waits for them, and re-layouts: 3.24 us -> 0 us
    pallas_call x1, Pallas kernels: 60.6 us -> 53.4 us  [local(): pl.pallas_call(kernel, out_shape=(jax.ShapeDtypeStruct((rows_dev, feature...]
    unnamed x2 -> x0, local copies, waits for them, and re-layouts: 3.24 us -> none
    pallas_call x0 -> x1, Pallas kernels: none -> 1.78 us  [local(): pl.pallas_call(deliver, out_shape=(jax.ShapeDtypeStruct(augmented.shape,...]
where the time goes in v2:
time: 56 us; the launch traced here: 55.8 us
  Pallas kernels  55.2 us (99%)
  between operations  0.64 us (1%)
    pallas_call x1, Pallas kernels, local(): pl.pallas_call(kernel, out_shape=(jax.ShapeDtypeStruct((rows_dev, feature...  53.4 us
    pallas_call x1, Pallas kernels, local(): pl.pallas_call(deliver, out_shape=(jax.ShapeDtypeStruct(augmented.shape,...  1.78 us

profile of v2, /device:TPU:1, one launch (start us, length us, event | category | flops | bytes accessed | tf_op | source)
XLA Modules:
  0.0 55.8 jit_solution(7358343613872126599)
XLA Ops:
  0.6 53.4 %expand_and_score.1 = (bf16[256,768]{1,0:T(8,128)(2,1)}, f32[32,4,128]{2,1,0:T(4,128)}) custom-call(bf16[256,768]{1,0:T(8,128)(2,1)} %db_hbm.1, s32[16,256]{1,0:T(8,128)} %bitcast.3, s32[1,256]{1,0:T(1,128)} %bitcast.4, bf16[16384,768]{1,0:T(8,128)(2,1)} %q_ref.1), custom_call_target="tpu_custom_call" | custom-call | tf_op jit(solution)/shard_map/expand_and_score/pallas_call | solution.py:408
  54.0 1.8 %deliver.1 = (bf16[256,768]{1,0:T(8,128)(2,1)}, f32[32,4,128]{2,1,0:T(4,128)}) custom-call(bf16[256,768]{1,0:T(8,128)(2,1)} %get-tuple-element.6.rows_in, f32[32,4,128]{2,1,0:T(4,128)} %get-tuple-element.7.best_in), custom_call_target="tpu_custom_call" | custom-call | tf_op jit(solution)/shard_map/deliver/pallas_call | solution.py:446

commit v3 on v2

--- a/solution.py
+++ b/solution.py
@@ -33,9 +33,9 @@
 def kernel(
     db_hbm, nb_hbm, vc_hbm, q_ref, aug_ref, best_ref,
     q_v, db_ref, nb_ref, vc_ref, pool, mask_ref, wanted, total, coded, coded_in, ranges, ranges_in, ranges_of,
-    everyone, first_top, tops, rivals, bases,
-    q_sem, l_sem, a_recv, b_recv, c_recv, p_recv, g_recv, s_recv, ab_send, c_send, r_send, r_recv,
-    p_send, g_send, s_send, m_send, m_recv, f_send, f_recv,
+    everyone, first_top, tops, y_in, y_best, z_in, bases,
+    q_sem, l_sem, a_recv, b_recv, c_recv, p_send, p_recv, g_recv, s_recv, y_recv, z_recv, ab_send,
+    c_send, r_send, r_recv, g_send, s_send, y_send, z_send, f_send, f_recv,
 ):
     rows_dev, features = db_ref.shape
     fanout = nb_ref.shape[0]
@@ -247,13 +247,17 @@
 
     def copy_p(dx, h):
         return remote(
-            coded.at[quarter(dx, h)], coded_in.at[h, dx - 1], p_send, p_recv.at[h], across(dx)
-        )
+            coded.at[quarter(dx, h)], coded_in.at[h, dx - 1], p_send.at[h], p_recv.at[h], across(dx)
+        )
+
+    def sent(ref, sem):
+        remote(ref, ref, sem, sem, sibling).wait_send()
 
     for dx in RING:
         copy_p(dx, 0).start()
     for dx in RING:
         copy_r(dx).start()
+    sent(coded_in.at[0], p_send.at[0])
     for dx in RING:
         copy_p(dx, 1).start()
 
@@ -266,17 +270,13 @@
         here = everyone.at[spot(h, 0, x)]
         return remote(here, here, g_send, g_recv.at[at], across(dx))
 
-    def copy_s(dx, h):
-        from_x = (x + SIDE - dx) % SIDE
-        return remote(
-            everyone.at[spot(h, 0, from_x)], everyone.at[spot(h, 1, from_x)], s_send,
+    def copy_s(h):
+        rows = SIDE * half
+        start = h * CORES * rows
+        return remote(
+            everyone.at[pl.ds(start, rows)], everyone.at[pl.ds(start + rows, rows)], s_send,
             s_recv.at[h], sibling,
         )
-
-    def sibling_rows(h):
-        start = (h * CORES + 1) * SIDE * half
-        here = everyone.at[pl.ds(start, SIDE * half)]
-        return remote(here, here, s_send, s_recv.at[h], sibling)
 
     sums = []
     for h in range(2):
@@ -290,104 +290,103 @@
     for h in range(2):
         summed = sums[h]
         here = coded_in.at[h]
-        remote(here, here, p_send, p_recv.at[h], sibling).wait_recv()
+        remote(here, here, p_send.at[h], p_recv.at[h], sibling).wait_recv()
         for dx in RING:
             part = coded_in[h, dx - 1].astype(jnp.float32)
             summed = summed + part * ranges_of[dx - 1, quarter(0, h), 0:1]
         everyone[spot(h, 0, x), :] = (summed * inverse_norm(summed)).astype(jnp.bfloat16)
         for dx in RING:
             copy_g(dx, h).start()
-        copy_s(0, h).start()
 
     def hand_over(h):
         for dx in RING:
             copy_g(dx, h).wait_recv()
-            copy_s(dx, h).start()
+        copy_s(h).start()
 
     hand_over(0)
     for load in query_loads:
         load.wait()
-    sibling_rows(0).wait_recv()
-
-    share = queries_here // CHIPS
+    copy_s(0).wait_recv()
+
+    shares = tops.shape[0]
+    share = queries_here // shares
     lines = share // 128
     part_rows = CORES * SIDE * half
 
-    def chip_at(k):
-        return (x, (chip + k) % CHIPS * CORES + c)
-
-    def copy_m(k):
-        return remote(tops.at[k], rivals.at[k], m_send, m_recv, chip_at(k))
-
     def folded_scores(h, k):
-        owner = (chip + k) % CHIPS
-        panel = q_v[pl.ds(pl.multiple_of(owner * share, share), share), :]
+        panel = q_v[pl.ds(k * share, share), :]
         scores = dot_rows(everyone[pl.ds(h * part_rows, part_rows), :], panel)
         return jnp.max(scores.reshape(part_rows // 8, 8, share), axis=0)
 
-    unroll = 4
-
-    def score_first(i, _):
-        for u in range(unroll):
-            k = (i * unroll + u + 1) % CHIPS
+    def score_first(begin, end):
+        for k in range(begin, end):
             first_top[k] = folded_scores(0, k)
-        return 0
-
-    def score_second(i, _):
-        for u in range(unroll):
-            k = (i * unroll + u + 1) % CHIPS
+
+    def score_second(begin, end):
+        for k in range(begin, end):
             top = jnp.maximum(first_top[k], folded_scores(1, k))
             top = jnp.max(top, axis=0, keepdims=True)
             for line in range(lines):
                 tops[k, pl.ds(line, 1), :] = top[:, line * 128 : (line + 1) * 128]
-        for u in range(unroll - 1):
-            copy_m(i * unroll + u + 1).start()
-
-        @pl.when(i < CHIPS // unroll - 1)
-        def _():
-            copy_m((i + 1) * unroll).start()
-
-        return 0
-
-    lax.fori_loop(0, 1, score_first, 0)
+
+    bounds = (0, shares * 3 // 4, shares)
+    spans = [pl.ds(begin, end - begin) for begin, end in zip(bounds[:-1], bounds[1:])]
+
+    def copy_y(i, n):
+        return remote(
+            tops.at[spans[n]], y_in.at[i, spans[n]], y_send, y_recv.at[n], plane(0, RING[i])
+        )
+
+    def copy_z(i, n):
+        return remote(
+            y_best.at[spans[n]], z_in.at[i, spans[n]], z_send, z_recv.at[n], plane(RING[i], 0)
+        )
+
+    def arrived(buffer, n, sem):
+        here = buffer.at[:, spans[n]]
+        remote(here, here, y_send, sem.at[n], sibling).wait_recv()
+
+    score_first(0, shares // 4)
     hand_over(1)
-    lax.fori_loop(1, CHIPS // unroll, score_first, 0)
-    sibling_rows(1).wait_recv()
-    lax.fori_loop(0, CHIPS // unroll, score_second, 0)
+    score_first(shares // 4, shares)
+    copy_s(1).wait_recv()
+    for n in range(2):
+        score_second(bounds[n], bounds[n + 1])
+        for i in range(SIDE - 1):
+            copy_y(i, n).start()
 
     for chip_x in range(SIDE):
         for h in range(2):
             start = h * part_rows + chip_x * half
             aug_ref[pl.ds(chip_x * own_rows + h * half, half), :] = everyone[pl.ds(start, half), :]
-    others = pl.ds(1, CHIPS - 1)
-    remote(tops.at[others], rivals.at[others], m_send, m_recv, sibling).wait_recv()
-    best = tops[0]
-    for k in range(1, CHIPS):
-        best = jnp.maximum(best, rivals[k])
-    here = c * CHIPS + chip
-    best_ref[here] = best
-    devices = CHIPS * CORES
-
-    def copy_f(k):
-        return remote(
-            best_ref.at[here], best_ref.at[here], f_send, f_recv, (x, (d + k) % devices)
-        )
-
-    for k in range(1, devices):
-        copy_f(k).start()
-
-    def sent(ref, sem):
-        remote(ref, ref, sem, sem, sibling).wait_send()
+
+    for n in range(2):
+        arrived(y_in, n, y_recv)
+        best = tops[spans[n]]
+        for i in range(SIDE - 1):
+            best = jnp.maximum(best, y_in[i, spans[n]])
+        y_best[spans[n]] = best
+        for i in range(SIDE - 1):
+            copy_z(i, n).start()
+    for n in range(2):
+        arrived(z_in, n, z_recv)
+        best = y_best[spans[n]]
+        for i in range(SIDE - 1):
+            best = jnp.maximum(best, z_in[i, spans[n]])
+        here = pl.ds(pl.multiple_of(c * shares, shares) + bounds[n], bounds[n + 1] - bounds[n])
+        best_ref[here] = best
+        remote(best_ref.at[here], best_ref.at[here], f_send, f_recv, sibling).start()
 
     sent(pool.at[pl.ds(0, 2 * (CHIPS - 1) * half)], ab_send)
     sent(pool.at[pl.ds(0, parity_rows)], c_send)
     sent(ranges_in, r_send)
-    sent(coded_in, p_send)
+    sent(coded_in.at[1], p_send.at[1])
     sent(everyone.at[pl.ds(0, 6 * half)], g_send)
     sent(everyone.at[pl.ds(0, 8 * half)], s_send)
-    sent(tops.at[others], m_send)
-    arrived = best_ref.at[pl.ds(0, devices - 1)]
-    remote(arrived, arrived, f_send, f_recv, sibling).wait()
+    sent(y_in, y_send)
+    sent(z_in, z_send)
+    here = best_ref.at[pl.ds(0, shares)]
+    remote(here, here, f_send, f_recv, sibling).wait()
 
 
 def deliver(rows_in, best_in, rows_out, best_out):
@@ -430,14 +429,16 @@
             pltpu.VMEM((CORES * rows_dev, features), jnp.bfloat16),
             pltpu.VMEM((CHIPS, 8, share), jnp.float32),
             pltpu.VMEM((CHIPS, share // 128, 128), jnp.float32),
+            pltpu.VMEM((SIDE - 1, CHIPS, share // 128, 128), jnp.float32),
             pltpu.VMEM((CHIPS, share // 128, 128), jnp.float32),
+            pltpu.VMEM((SIDE - 1, CHIPS, share // 128, 128), jnp.float32),
             pltpu.SMEM((CHIPS * CORES,), jnp.int32),
             dma((4,)),
             dma((4,)),
         ]
         + [dma((CHIPS,))] * 2
-        + [dma((4,)), dma((2,)), dma((2 * SIDE,)), dma((2,))]
-        + [dma] * 11,
+        + [dma((4,)), dma((2,)), dma((2,)), dma((2 * SIDE,)), dma((2,)), dma((2,)), dma((2,))]
+        + [dma] * 10,
         compiler_params=pltpu.CompilerParams(
             collective_id=0, has_side_effects=True, vmem_limit_bytes=56 * 2**20
         ),

time: 56 us -> 53.8 us (0.961)
  Pallas kernels: 55.2 us -> 53 us
    pallas_call x1, Pallas kernels: 53.4 us -> 51.3 us  [local(): pl.pallas_call(kernel, out_shape=(jax.ShapeDtypeStruct((rows_dev, feature...]
where the time goes in v3:
time: 53.8 us; the launch traced here: 53.7 us
  Pallas kernels  53 us (99%)
  between operations  0.64 us (1%)
    pallas_call x1, Pallas kernels, local(): pl.pallas_call(kernel, out_shape=(jax.ShapeDtypeStruct((rows_dev, feature...  51.3 us
    pallas_call x1, Pallas kernels, local(): pl.pallas_call(deliver, out_shape=(jax.ShapeDtypeStruct(augmented.shape,...  1.78 us

profile of v3, /device:TPU:1, one launch (start us, length us, event | category | flops | bytes accessed | tf_op | source)
XLA Modules:
  0.0 53.7 jit_solution(3558352731784399282)
XLA Ops:
  0.6 51.3 %expand_and_score.1 = (bf16[256,768]{1,0:T(8,128)(2,1)}, f32[32,4,128]{2,1,0:T(4,128)}) custom-call(bf16[256,768]{1,0:T(8,128)(2,1)} %db_hbm.1, s32[16,256]{1,0:T(8,128)} %bitcast.3, s32[1,256]{1,0:T(1,128)} %bitcast.4, bf16[16384,768]{1,0:T(8,128)(2,1)} %q_ref.1), custom_call_target="tpu_custom_call" | custom-call | tf_op jit(solution)/shard_map/expand_and_score/pallas_call | solution.py:407
  51.9 1.8 %deliver.1 = (bf16[256,768]{1,0:T(8,128)(2,1)}, f32[32,4,128]{2,1,0:T(4,128)}) custom-call(bf16[256,768]{1,0:T(8,128)(2,1)} %get-tuple-element.6.rows_in, f32[32,4,128]{2,1,0:T(4,128)} %get-tuple-element.7.best_in), custom_call_target="tpu_custom_call" | custom-call | tf_op jit(solution)/shard_map/deliver/pallas_call | solution.py:447

commit v4 on v3

--- a/solution.py
+++ b/solution.py
@@ -32,7 +32,7 @@
 
 def kernel(
     db_hbm, nb_hbm, vc_hbm, q_ref, aug_ref, best_ref,
-    q_v, db_ref, nb_ref, vc_ref, pool, mask_ref, wanted, total, coded, coded_in, ranges, ranges_in, ranges_of,
+    q_v, q_t, db_ref, nb_ref, vc_ref, pool, mask_ref, wanted, total, coded, coded_in, ranges, ranges_in, ranges_of,
     everyone, first_top, tops, y_in, y_best, z_in, bases,
     q_sem, l_sem, a_recv, b_recv, c_recv, p_send, p_recv, g_recv, s_recv, y_recv, z_recv, ab_send,
     c_send, r_send, r_recv, g_send, s_send, y_send, z_send, f_send, f_recv,
@@ -239,7 +239,7 @@
     ranges[...] = spread_range.T[0:8, :]
 
     def quarter(dx, h):
-        start = (x + dx) % SIDE * own_rows + h * half
+        start = (x + SIDE + dx) % SIDE * own_rows + h * half
         return pl.ds(pl.multiple_of(start, half), half)
 
     def copy_r(dx):
@@ -257,25 +257,37 @@
         copy_p(dx, 0).start()
     for dx in RING:
         copy_r(dx).start()
+    for load in query_loads:
+        load.wait()
+    panel_rows = 512
+
+    def turn(i, _):
+        for u in range(4):
+            rows = pl.ds(pl.multiple_of((i * 4 + u) * panel_rows, panel_rows), panel_rows)
+            q_t[:, rows] = q_v[rows, :].T
+        return 0
+
+    turns = queries_here // (4 * panel_rows)
+    lax.fori_loop(0, turns // 2, turn, 0)
     sent(coded_in.at[0], p_send.at[0])
     for dx in RING:
         copy_p(dx, 1).start()
-
-    def spot(h, core, chip_x):
-        start = (h * CORES + core) * SIDE * half + chip_x * half
-        return pl.ds(pl.multiple_of(start, half), half)
-
-    def copy_g(dx, h):
-        at = h * SIDE + dx
-        here = everyone.at[spot(h, 0, x)]
-        return remote(here, here, g_send, g_recv.at[at], across(dx))
-
-    def copy_s(h):
-        rows = SIDE * half
-        start = h * CORES * rows
-        return remote(
-            everyone.at[pl.ds(start, rows)], everyone.at[pl.ds(start + rows, rows)], s_send,
-            s_recv.at[h], sibling,
+    lax.fori_loop(turns // 2, turns, turn, 0)
+
+    others = (SIDE - 1) * half
+    starts = (0, 2 * own_rows, 2 * own_rows + 2 * others)
+    sizes = (own_rows, others, others)
+
+    def copy_g(i, h):
+        return remote(
+            everyone.at[pl.ds(h * half, half)], everyone.at[pl.ds(starts[1 + h] + i * half, half)],
+            g_send, g_recv.at[h], across(RING[i]),
+        )
+
+    def copy_s(n):
+        return remote(
+            everyone.at[pl.ds(starts[n], sizes[n])],
+            everyone.at[pl.ds(starts[n] + sizes[n], sizes[n])], s_send, s_recv.at[n], sibling,
         )
 
     sums = []
@@ -294,37 +306,29 @@
         for dx in RING:
             part = coded_in[h, dx - 1].astype(jnp.float32)
             summed = summed + part * ranges_of[dx - 1, quarter(0, h), 0:1]
-        everyone[spot(h, 0, x), :] = (summed * inverse_norm(summed)).astype(jnp.bfloat16)
-        for dx in RING:
-            copy_g(dx, h).start()
+        everyone[pl.ds(h * half, half), :] = (summed * inverse_norm(summed)).astype(jnp.bfloat16)
+        for i in range(SIDE - 1):
+            copy_g(i, h).start()
+    copy_s(0).start()
 
     def hand_over(h):
-        for dx in RING:
-            copy_g(dx, h).wait_recv()
-        copy_s(h).start()
-
-    hand_over(0)
-    for load in query_loads:
-        load.wait()
-    copy_s(0).wait_recv()
+        here = everyone.at[pl.ds(starts[1 + h], others)]
+        remote(here, here, g_send, g_recv.at[h], sibling).wait_recv()
+        copy_s(1 + h).start()
 
     shares = tops.shape[0]
     share = queries_here // shares
     lines = share // 128
-    part_rows = CORES * SIDE * half
-
-    def folded_scores(h, k):
-        panel = q_v[pl.ds(k * share, share), :]
-        scores = dot_rows(everyone[pl.ds(h * part_rows, part_rows), :], panel)
-        return jnp.max(scores.reshape(part_rows // 8, 8, share), axis=0)
-
-    def score_first(begin, end):
+
+    def folded_scores(n, k):
+        rows = everyone[pl.ds(starts[n], 2 * sizes[n]), :]
+        panel = q_t[:, pl.ds(k * share, share)]
+        scores = jnp.dot(rows, panel, preferred_element_type=jnp.float32)
+        return jnp.max(scores.reshape(2 * sizes[n] // 8, 8, share), axis=0)
+
+    def score_last(begin, end):
         for k in range(begin, end):
-            first_top[k] = folded_scores(0, k)
-
-    def score_second(begin, end):
-        for k in range(begin, end):
-            top = jnp.maximum(first_top[k], folded_scores(1, k))
+            top = jnp.maximum(first_top[k], folded_scores(2, k))
             top = jnp.max(top, axis=0, keepdims=True)
             for line in range(lines):
                 tops[k, pl.ds(line, 1), :] = top[:, line * 128 : (line + 1) * 128]
@@ -346,19 +350,27 @@
         here = buffer.at[:, spans[n]]
         remote(here, here, y_send, sem.at[n], sibling).wait_recv()
 
-    score_first(0, shares // 4)
+    copy_s(0).wait_recv()
+    for k in range(shares):
+        first_top[k] = folded_scores(0, k)
+    hand_over(0)
+    copy_s(1).wait_recv()
+    for k in range(shares // 2):
+        first_top[k] = jnp.maximum(first_top[k], folded_scores(1, k))
     hand_over(1)
-    score_first(shares // 4, shares)
-    copy_s(1).wait_recv()
+    for k in range(shares // 2, shares):
+        first_top[k] = jnp.maximum(first_top[k], folded_scores(1, k))
+    copy_s(2).wait_recv()
     for n in range(2):
-        score_second(bounds[n], bounds[n + 1])
+        score_last(bounds[n], bounds[n + 1])
         for i in range(SIDE - 1):
             copy_y(i, n).start()
 
-    for chip_x in range(SIDE):
-        for h in range(2):
-            start = h * part_rows + chip_x * half
-            aug_ref[pl.ds(chip_x * own_rows + h * half, half), :] = everyone[pl.ds(start, half), :]
+    aug_ref[pl.ds(mine, own_rows), :] = everyone[pl.ds(0, own_rows), :]
+    for h in range(2):
+        for i in range(SIDE - 1):
+            start = starts[1 + h] + i * half
+            aug_ref[quarter(-RING[i], h), :] = everyone[pl.ds(start, half), :]
 
     for n in range(2):
         arrived(y_in, n, y_recv)
@@ -414,6 +426,7 @@
         out_specs=(vmem, vmem),
         scratch_shapes=[
             pltpu.VMEM((queries_here, features), jnp.bfloat16),
+            pltpu.VMEM((features, queries_here), jnp.bfloat16),
             pltpu.VMEM((rows_dev, features), jnp.bfloat16),
             pltpu.VMEM((fanout, rows_dev), jnp.int32),
             pltpu.VMEM((1, rows_dev), jnp.int32),
@@ -437,7 +450,7 @@
             dma((4,)),
         ]
         + [dma((CHIPS,))] * 2
-        + [dma((4,)), dma((2,)), dma((2,)), dma((2 * SIDE,)), dma((2,)), dma((2,)), dma((2,))]
+        + [dma((4,)), dma((2,)), dma((2,)), dma((2,)), dma((3,)), dma((2,)), dma((2,))]
         + [dma] * 10,
         compiler_params=pltpu.CompilerParams(
             collective_id=0, has_side_effects=True, vmem_limit_bytes=56 * 2**20

time: 53.8 us -> 53.1 us (0.987)
  Pallas kernels: 53 us -> 52.3 us
    pallas_call x1, Pallas kernels: 51.3 us -> 50.5 us  [local(): pl.pallas_call(kernel, out_shape=(jax.ShapeDtypeStruct((rows_dev, feature...]
where the time goes in v4:
time: 53.1 us; the launch traced here: 53 us
  Pallas kernels  52.3 us (98%)
  between operations  0.64 us (1%)
    pallas_call x1, Pallas kernels, local(): pl.pallas_call(kernel, out_shape=(jax.ShapeDtypeStruct((rows_dev, feature...  50.5 us
    pallas_call x1, Pallas kernels, local(): pl.pallas_call(deliver, out_shape=(jax.ShapeDtypeStruct(augmented.shape,...  1.78 us

profile of v4, /device:TPU:1, one launch (start us, length us, event | category | flops | bytes accessed | tf_op | source)
XLA Modules:
  0.0 53.0 jit_solution(8943312587870282975)
XLA Ops:
  0.6 50.5 %expand_and_score.1 = (bf16[256,768]{1,0:T(8,128)(2,1)}, f32[32,4,128]{2,1,0:T(4,128)}) custom-call(bf16[256,768]{1,0:T(8,128)(2,1)} %db_hbm.1, s32[16,256]{1,0:T(8,128)} %bitcast.3, s32[1,256]{1,0:T(1,128)} %bitcast.4, bf16[16384,768]{1,0:T(8,128)(2,1)} %q_ref.1), custom_call_target="tpu_custom_call" | custom-call | tf_op jit(solution)/shard_map/expand_and_score/pallas_call | solution.py:419
  51.2 1.8 %deliver.1 = (bf16[256,768]{1,0:T(8,128)(2,1)}, f32[32,4,128]{2,1,0:T(4,128)}) custom-call(bf16[256,768]{1,0:T(8,128)(2,1)} %get-tuple-element.6.rows_in, f32[32,4,128]{2,1,0:T(4,128)} %get-tuple-element.7.best_in), custom_call_target="tpu_custom_call" | custom-call | tf_op jit(solution)/shard_map/deliver/pallas_call | solution.py:460

commit v5 on v4

--- a/solution.py
+++ b/solution.py
@@ -18,6 +18,7 @@
 )
 SLOT_AT = {offset: place for place, offset in enumerate(SLOTS)}
 RING = (1, 3, 2)
+FAR_FIRST = (2, 1, 3)
 
 
 def inverse_norm(values):
@@ -35,7 +36,7 @@
     q_v, q_t, db_ref, nb_ref, vc_ref, pool, mask_ref, wanted, total, coded, coded_in, ranges, ranges_in, ranges_of,
     everyone, first_top, tops, y_in, y_best, z_in, bases,
     q_sem, l_sem, a_recv, b_recv, c_recv, p_send, p_recv, g_recv, s_recv, y_recv, z_recv, ab_send,
-    c_send, r_send, r_recv, g_send, s_send, y_send, z_send, f_send, f_recv,
+    c_send, r_send, r_recv, g_send, s_send, y_send, z_send,
 ):
     rows_dev, features = db_ref.shape
     fanout = nb_ref.shape[0]
@@ -219,7 +220,12 @@
         @pl.when((i == 4) | (i == 5))
         def _():
             for u in range(4):
-                pass_on(part * 4 + u)
+                here = block(part * 4 + u, 0, 0, own_rows)
+                remote(here, here, ab_send, a_recv.at[part * 4 + u], sibling).wait_recv()
+            remote(
+                block(part * 4, 0, 0, span), block(part * 4, 1, 0, span), c_send,
+                c_recv.at[part], sibling,
+            ).start()
 
         @pl.when(part >= 4)
         def _():
@@ -253,9 +259,9 @@
     def sent(ref, sem):
         remote(ref, ref, sem, sem, sibling).wait_send()
 
-    for dx in RING:
+    for dx in FAR_FIRST:
         copy_p(dx, 0).start()
-    for dx in RING:
+    for dx in FAR_FIRST:
         copy_r(dx).start()
     for load in query_loads:
         load.wait()
@@ -270,7 +276,7 @@
     turns = queries_here // (4 * panel_rows)
     lax.fori_loop(0, turns // 2, turn, 0)
     sent(coded_in.at[0], p_send.at[0])
-    for dx in RING:
+    for dx in FAR_FIRST:
         copy_p(dx, 1).start()
     lax.fori_loop(turns // 2, turns, turn, 0)
 
@@ -281,7 +287,7 @@
     def copy_g(i, h):
         return remote(
             everyone.at[pl.ds(h * half, half)], everyone.at[pl.ds(starts[1 + h] + i * half, half)],
-            g_send, g_recv.at[h], across(RING[i]),
+            g_send, g_recv.at[h], across(FAR_FIRST[i]),
         )
 
     def copy_s(n):
@@ -295,7 +301,7 @@
         kept = db_ref[quarter(0, h), :].astype(jnp.float32)
         sums.append(kept * inverse_norm(kept) + total[quarter(0, h), :])
     remote(ranges_in, ranges_in, r_send, r_recv, sibling).wait_recv()
-    for dx in RING:
+    for dx in FAR_FIRST:
         across_range = jnp.broadcast_to(ranges_in[dx - 1, 0:1, :], (128, rows_dev))
         ranges_of[dx - 1] = across_range.T
 
@@ -303,7 +309,7 @@
         summed = sums[h]
         here = coded_in.at[h]
         remote(here, here, p_send.at[h], p_recv.at[h], sibling).wait_recv()
-        for dx in RING:
+        for dx in FAR_FIRST:
             part = coded_in[h, dx - 1].astype(jnp.float32)
             summed = summed + part * ranges_of[dx - 1, quarter(0, h), 0:1]
         everyone[pl.ds(h * half, half), :] = (summed * inverse_norm(summed)).astype(jnp.bfloat16)
@@ -338,12 +344,16 @@
 
     def copy_y(i, n):
         return remote(
-            tops.at[spans[n]], y_in.at[i, spans[n]], y_send, y_recv.at[n], plane(0, RING[i])
-        )
-
-    def copy_z(i, n):
-        return remote(
-            y_best.at[spans[n]], z_in.at[i, spans[n]], z_send, z_recv.at[n], plane(RING[i], 0)
+            tops.at[spans[n]], y_in.at[i, spans[n]], y_send, y_recv.at[n], plane(0, FAR_FIRST[i])
+        )
+
+    def copy_z(i, n, other):
+        to_x, to_d = plane(FAR_FIRST[i], 0)
+        if other:
+            to_d = to_d + 1 - 2 * c
+        return remote(
+            y_best.at[spans[n]], z_in.at[other * (SIDE - 1) + i, spans[n]], z_send, z_recv.at[n],
+            (to_x, to_d),
         )
 
     def arrived(buffer, n, sem):
@@ -351,9 +361,11 @@
         remote(here, here, y_send, sem.at[n], sibling).wait_recv()
 
     copy_s(0).wait_recv()
-    for k in range(shares):
+    for k in range(12):
         first_top[k] = folded_scores(0, k)
     hand_over(0)
+    for k in range(12, shares):
+        first_top[k] = folded_scores(0, k)
     copy_s(1).wait_recv()
     for k in range(shares // 2):
         first_top[k] = jnp.maximum(first_top[k], folded_scores(1, k))
@@ -370,7 +382,7 @@
     for h in range(2):
         for i in range(SIDE - 1):
             start = starts[1 + h] + i * half
-            aug_ref[quarter(-RING[i], h), :] = everyone[pl.ds(start, half), :]
+            aug_ref[quarter(-FAR_FIRST[i], h), :] = everyone[pl.ds(start, half), :]
 
     for n in range(2):
         arrived(y_in, n, y_recv)
@@ -378,16 +390,21 @@
         for i in range(SIDE - 1):
             best = jnp.maximum(best, y_in[i, spans[n]])
         y_best[spans[n]] = best
-        for i in range(SIDE - 1):
-            copy_z(i, n).start()
+        for other in range(CORES):
+            for i in range(SIDE - 1):
+                copy_z(i, n, other).start()
+        remote(
+            y_best.at[spans[n]], z_in.at[2 * (SIDE - 1), spans[n]], z_send, z_recv.at[n], sibling
+        ).start()
     for n in range(2):
         arrived(z_in, n, z_recv)
-        best = y_best[spans[n]]
-        for i in range(SIDE - 1):
-            best = jnp.maximum(best, z_in[i, spans[n]])
-        here = pl.ds(pl.multiple_of(c * shares, shares) + bounds[n], bounds[n + 1] - bounds[n])
-        best_ref[here] = best
-        remote(best_ref.at[here], best_ref.at[here], f_send, f_recv, sibling).start()
+        for other in range(CORES):
+            best = z_in[2 * (SIDE - 1), spans[n]] if other else y_best[spans[n]]
+            for i in range(SIDE - 1):
+                best = jnp.maximum(best, z_in[other * (SIDE - 1) + i, spans[n]])
+            first = (1 - c if other else c) * shares
+            here = pl.ds(pl.multiple_of(first, shares) + bounds[n], bounds[n + 1] - bounds[n])
+            best_ref[here] = best
 
     sent(pool.at[pl.ds(0, 2 * (CHIPS - 1) * half)], ab_send)
     sent(pool.at[pl.ds(0, parity_rows)], c_send)
@@ -397,8 +414,6 @@
     sent(everyone.at[pl.ds(0, 8 * half)], s_send)
     sent(y_in, y_send)
     sent(z_in, z_send)
-    here = best_ref.at[pl.ds(0, shares)]
-    remote(here, here, f_send, f_recv, sibling).wait()
 
 
 def deliver(rows_in, best_in, rows_out, best_out):
@@ -419,8 +434,8 @@
     augmented, best = pl.pallas_call(
         kernel,
         out_shape=(
-            jax.ShapeDtypeStruct((rows_dev, features), jnp.bfloat16),
-            jax.ShapeDtypeStruct((CORES * CHIPS, share // 128, 128), jnp.float32),
+            pltpu.VMEM((rows_dev, features), jnp.bfloat16),
+            pltpu.VMEM((CORES * CHIPS, share // 128, 128), jnp.float32),
         ),
         in_specs=[anywhere, anywhere, anywhere, anywhere],
         out_specs=(vmem, vmem),
@@ -444,14 +459,14 @@
             pltpu.VMEM((CHIPS, share // 128, 128), jnp.float32),
             pltpu.VMEM((SIDE - 1, CHIPS, share // 128, 128), jnp.float32),
             pltpu.VMEM((CHIPS, share // 128, 128), jnp.float32),
-            pltpu.VMEM((SIDE - 1, CHIPS, share // 128, 128), jnp.float32),
+            pltpu.VMEM((2 * SIDE - 1, CHIPS, share // 128, 128), jnp.float32),
             pltpu.SMEM((CHIPS * CORES,), jnp.int32),
             dma((4,)),
             dma((4,)),
         ]
         + [dma((CHIPS,))] * 2
         + [dma((4,)), dma((2,)), dma((2,)), dma((2,)), dma((3,)), dma((2,)), dma((2,))]
-        + [dma] * 10,
+        + [dma] * 8,
         compiler_params=pltpu.CompilerParams(
             collective_id=0, has_side_effects=True, vmem_limit_bytes=56 * 2**20
         ),
@@ -466,7 +481,10 @@
         in_specs=[vmem, vmem],
         out_specs=(vmem, vmem),
         name="deliver",
-    )(augmented, best)
+    )(
+        pltpu.with_memory_space_constraint(augmented, pltpu.VMEM),
+        pltpu.with_memory_space_constraint(best, pltpu.VMEM),
+    )
     return augmented, best.reshape(queries.shape[0])
 
 

time: 53.1 us -> 50.4 us (0.949)
  Pallas kernels: 52.3 us -> 49.7 us
    pallas_call x1, Pallas kernels: 50.5 us -> 48.9 us  [local(): pl.pallas_call(kernel, out_shape=(pltpu.VMEM((rows_dev, features), jnp.bf...]
    pallas_call x1, Pallas kernels: 1.78 us -> 0.79 us  [local(): pl.pallas_call(deliver, out_shape=(jax.ShapeDtypeStruct(augmented.shape,...]
where the time goes in v5:
time: 50.4 us; the launch traced here: 50.3 us
  Pallas kernels  49.7 us (99%)
  between operations  0.64 us (1%)
    pallas_call x1, Pallas kernels, local(): pl.pallas_call(kernel, out_shape=(pltpu.VMEM((rows_dev, features), jnp.bf...  48.9 us

profile of v5, /device:TPU:1, one launch (start us, length us, event | category | flops | bytes accessed | tf_op | source)
XLA Modules:
  0.0 50.3 jit_solution(14663388542066730432)
XLA Ops:
  0.6 48.9 %expand_and_score.1 = (bf16[256,768]{1,0:T(8,128)(2,1)S(1)}, f32[32,4,128]{2,1,0:T(4,128)S(1)}) custom-call(bf16[256,768]{1,0:T(8,128)(2,1)} %db_hbm.1, s32[16,256]{1,0:T(8,128)} %bitcast.3, s32[1,256]{1,0:T(1,128)} %bitcast.4, bf16[16384,768]{1,0:T(8,128)(2,1)} %q_ref.1), custom_call_target="tpu_custom_call" | custom-call | tf_op jit(solution)/shard_map/expand_and_score/pallas_call | solution.py:434
  49.5 0.8 %deliver.1 = (bf16[256,768]{1,0:T(8,128)(2,1)}, f32[32,4,128]{2,1,0:T(4,128)}) custom-call(bf16[256,768]{1,0:T(8,128)(2,1)S(1)} %get-tuple-element.6.rows_in, f32[32,4,128]{2,1,0:T(4,128)S(1)} %get-tuple-element.7.best_in), custom_call_target="tpu_custom_call" | custom-call | tf_op jit(solution)/shard_map/deliver/pallas_call | solution.py:475

commit v6 on v5

--- a/solution.py
+++ b/solution.py
@@ -19,6 +19,7 @@
 SLOT_AT = {offset: place for place, offset in enumerate(SLOTS)}
 RING = (1, 3, 2)
 FAR_FIRST = (2, 1, 3)
+EARLY = 12
 
 
 def inverse_norm(values):
@@ -34,9 +35,9 @@
 def kernel(
     db_hbm, nb_hbm, vc_hbm, q_ref, aug_ref, best_ref,
     q_v, q_t, db_ref, nb_ref, vc_ref, pool, mask_ref, wanted, total, coded, coded_in, ranges, ranges_in, ranges_of,
-    everyone, first_top, tops, y_in, y_best, z_in, bases,
-    q_sem, l_sem, a_recv, b_recv, c_recv, p_send, p_recv, g_recv, s_recv, y_recv, z_recv, ab_send,
-    c_send, r_send, r_recv, g_send, s_send, y_send, z_send,
+    everyone, first_top, tops, y_in, y_best, z_in, late_in, bases,
+    q_sem, l_sem, a_recv, b_recv, c_recv, p_send, p_recv, g_recv, s_recv, ab_send, c_send,
+    r_send, r_recv, g_send, s_send, y_send, y_recv, z_send, z_recv, t_send, t_recv, f_send, f_recv,
 ):
     rows_dev, features = db_ref.shape
     fanout = nb_ref.shape[0]
@@ -326,57 +327,75 @@
     share = queries_here // shares
     lines = share // 128
 
-    def folded_scores(n, k):
-        rows = everyone[pl.ds(starts[n], 2 * sizes[n]), :]
+    def folded_scores(begin, end, k):
         panel = q_t[:, pl.ds(k * share, share)]
-        scores = jnp.dot(rows, panel, preferred_element_type=jnp.float32)
-        return jnp.max(scores.reshape(2 * sizes[n] // 8, 8, share), axis=0)
-
-    def score_last(begin, end):
-        for k in range(begin, end):
-            top = jnp.maximum(first_top[k], folded_scores(2, k))
-            top = jnp.max(top, axis=0, keepdims=True)
-            for line in range(lines):
-                tops[k, pl.ds(line, 1), :] = top[:, line * 128 : (line + 1) * 128]
-
-    bounds = (0, shares * 3 // 4, shares)
-    spans = [pl.ds(begin, end - begin) for begin, end in zip(bounds[:-1], bounds[1:])]
-
-    def copy_y(i, n):
-        return remote(
-            tops.at[spans[n]], y_in.at[i, spans[n]], y_send, y_recv.at[n], plane(0, FAR_FIRST[i])
-        )
-
-    def copy_z(i, n, other):
+        scores = jnp.dot(
+            everyone[pl.ds(begin, end - begin), :], panel, preferred_element_type=jnp.float32
+        )
+        return jnp.max(scores.reshape((end - begin) // 8, 8, share), axis=0)
+
+    first, second, third = starts
+    stop = 2 * rows_dev
+
+    def finish(k, begin):
+        top = jnp.maximum(first_top[k], folded_scores(begin, stop, k))
+        top = jnp.max(top, axis=0, keepdims=True)
+        for line in range(lines):
+            tops[k, pl.ds(line, 1), :] = top[:, line * 128 : (line + 1) * 128]
+
+    early = y_best.shape[0]
+    early_shares, late_shares = pl.ds(0, early), pl.ds(early, shares - early)
+
+    def copy_y(i):
+        return remote(
+            tops.at[early_shares], y_in.at[i], y_send, y_recv, plane(0, FAR_FIRST[i])
+        )
+
+    def copy_z(i, other):
         to_x, to_d = plane(FAR_FIRST[i], 0)
         if other:
             to_d = to_d + 1 - 2 * c
         return remote(
-            y_best.at[spans[n]], z_in.at[other * (SIDE - 1) + i, spans[n]], z_send, z_recv.at[n],
-            (to_x, to_d),
-        )
-
-    def arrived(buffer, n, sem):
-        here = buffer.at[:, spans[n]]
-        remote(here, here, y_send, sem.at[n], sibling).wait_recv()
+            y_best, z_in.at[other * (SIDE - 1) + i], z_send, z_recv, (to_x, to_d)
+        )
+
+    def copy_l(place):
+        return remote(
+            tops.at[late_shares], late_in.at[place - 1], t_send, t_recv, plane(*SLOTS[place])
+        )
+
+    def arrived(buffer, sem):
+        remote(buffer, buffer, y_send, sem, sibling).wait_recv()
 
     copy_s(0).wait_recv()
-    for k in range(12):
-        first_top[k] = folded_scores(0, k)
-    hand_over(0)
-    for k in range(12, shares):
-        first_top[k] = folded_scores(0, k)
+    for k in range(shares):
+        if k == shares * 3 // 4:
+            hand_over(0)
+        first_top[k] = folded_scores(first, second, k)
     copy_s(1).wait_recv()
-    for k in range(shares // 2):
-        first_top[k] = jnp.maximum(first_top[k], folded_scores(1, k))
-    hand_over(1)
-    for k in range(shares // 2, shares):
-        first_top[k] = jnp.maximum(first_top[k], folded_scores(1, k))
+    for k in range(early):
+        if k == early // 2:
+            hand_over(1)
+        first_top[k] = jnp.maximum(first_top[k], folded_scores(second, third, k))
     copy_s(2).wait_recv()
-    for n in range(2):
-        score_last(bounds[n], bounds[n + 1])
+    for k in range(early):
+        finish(k, third)
+    for i in range(SIDE - 1):
+        copy_y(i).start()
+    for k in range(early, shares):
+        finish(k, second)
+    for place in reversed(range(1, CHIPS)):
+        copy_l(place).start()
+
+    arrived(y_in, y_recv)
+    best = tops[early_shares]
+    for i in range(SIDE - 1):
+        best = jnp.maximum(best, y_in[i])
+    y_best[...] = best
+    for other in range(CORES):
         for i in range(SIDE - 1):
-            copy_y(i, n).start()
+            copy_z(i, other).start()
+    remote(y_best, z_in.at[2 * (SIDE - 1)], z_send, z_recv, sibling).start()
 
     aug_ref[pl.ds(mine, own_rows), :] = everyone[pl.ds(0, own_rows), :]
     for h in range(2):
@@ -384,27 +403,22 @@
             start = starts[1 + h] + i * half
             aug_ref[quarter(-FAR_FIRST[i], h), :] = everyone[pl.ds(start, half), :]
 
-    for n in range(2):
-        arrived(y_in, n, y_recv)
-        best = tops[spans[n]]
+    arrived(late_in, t_recv)
+    best = tops[late_shares]
+    for i in range(CHIPS - 1):
+        best = jnp.maximum(best, late_in[i])
+    here = pl.ds(pl.multiple_of(c * shares, shares) + early, shares - early)
+    best_ref[here] = best
+    copy_f = remote(best_ref.at[here], best_ref.at[here], f_send, f_recv, sibling)
+    copy_f.start()
+
+    arrived(z_in, z_recv)
+    for other in range(CORES):
+        best = z_in[2 * (SIDE - 1)] if other else y_best[...]
         for i in range(SIDE - 1):
-            best = jnp.maximum(best, y_in[i, spans[n]])
-        y_best[spans[n]] = best
-        for other in range(CORES):
-            for i in range(SIDE - 1):
-                copy_z(i, n, other).start()
-        remote(
-            y_best.at[spans[n]], z_in.at[2 * (SIDE - 1), spans[n]], z_send, z_recv.at[n], sibling
-        ).start()
-    for n in range(2):
-        arrived(z_in, n, z_recv)
-        for other in range(CORES):
-            best = z_in[2 * (SIDE - 1), spans[n]] if other else y_best[spans[n]]
-            for i in range(SIDE - 1):
-                best = jnp.maximum(best, z_in[other * (SIDE - 1) + i, spans[n]])
-            first = (1 - c if other else c) * shares
-            here = pl.ds(pl.multiple_of(first, shares) + bounds[n], bounds[n + 1] - bounds[n])
-            best_ref[here] = best
+            best = jnp.maximum(best, z_in[other * (SIDE - 1) + i])
+        start = (1 - c if other else c) * shares
+        best_ref[pl.ds(pl.multiple_of(start, shares), early)] = best
 
     sent(pool.at[pl.ds(0, 2 * (CHIPS - 1) * half)], ab_send)
     sent(pool.at[pl.ds(0, parity_rows)], c_send)
@@ -414,6 +428,8 @@
     sent(everyone.at[pl.ds(0, 8 * half)], s_send)
     sent(y_in, y_send)
     sent(z_in, z_send)
+    sent(late_in, t_send)
+    copy_f.wait()
 
 
 def deliver(rows_in, best_in, rows_out, best_out):
@@ -457,16 +473,17 @@
             pltpu.VMEM((CORES * rows_dev, features), jnp.bfloat16),
             pltpu.VMEM((CHIPS, 8, share), jnp.float32),
             pltpu.VMEM((CHIPS, share // 128, 128), jnp.float32),
-            pltpu.VMEM((SIDE - 1, CHIPS, share // 128, 128), jnp.float32),
-            pltpu.VMEM((CHIPS, share // 128, 128), jnp.float32),
-            pltpu.VMEM((2 * SIDE - 1, CHIPS, share // 128, 128), jnp.float32),
+            pltpu.VMEM((SIDE - 1, EARLY, share // 128, 128), jnp.float32),
+            pltpu.VMEM((EARLY, share // 128, 128), jnp.float32),
+            pltpu.VMEM((2 * SIDE - 1, EARLY, share // 128, 128), jnp.float32),
+            pltpu.VMEM((CHIPS - 1, CHIPS - EARLY, share // 128, 128), jnp.float32),
             pltpu.SMEM((CHIPS * CORES,), jnp.int32),
             dma((4,)),
             dma((4,)),
         ]
         + [dma((CHIPS,))] * 2
-        + [dma((4,)), dma((2,)), dma((2,)), dma((2,)), dma((3,)), dma((2,)), dma((2,))]
-        + [dma] * 8,
+        + [dma((4,)), dma((2,)), dma((2,)), dma((2,)), dma((3,))]
+        + [dma] * 14,
         compiler_params=pltpu.CompilerParams(
             collective_id=0, has_side_effects=True, vmem_limit_bytes=56 * 2**20
         ),

time: 50.4 us -> 49.3 us (0.978)
  Pallas kernels: 49.7 us -> 48.5 us
    pallas_call x1, Pallas kernels: 48.9 us -> 47.7 us  [local(): pl.pallas_call(kernel, out_shape=(pltpu.VMEM((rows_dev, features), jnp.bf...]
where the time goes in v6:
time: 49.3 us; the launch traced here: 49.2 us
  Pallas kernels  48.5 us (98%)
  between operations  0.64 us (1%)
    pallas_call x1, Pallas kernels, local(): pl.pallas_call(kernel, out_shape=(pltpu.VMEM((rows_dev, features), jnp.bf...  47.7 us

profile of v6, /device:TPU:1, one launch (start us, length us, event | category | flops | bytes accessed | tf_op | source)
XLA Modules:
  0.0 49.2 jit_solution(17785669003173448817)
XLA Ops:
  0.6 47.7 %expand_and_score.1 = (bf16[256,768]{1,0:T(8,128)(2,1)S(1)}, f32[32,4,128]{2,1,0:T(4,128)S(1)}) custom-call(bf16[256,768]{1,0:T(8,128)(2,1)} %db_hbm.1, s32[16,256]{1,0:T(8,128)} %bitcast.3, s32[1,256]{1,0:T(1,128)} %bitcast.4, bf16[16384,768]{1,0:T(8,128)(2,1)} %q_ref.1), custom_call_target="tpu_custom_call" | custom-call | tf_op jit(solution)/shard_map/expand_and_score/pallas_call | solution.py:450
  48.4 0.8 %deliver.1 = (bf16[256,768]{1,0:T(8,128)(2,1)}, f32[32,4,128]{2,1,0:T(4,128)}) custom-call(bf16[256,768]{1,0:T(8,128)(2,1)S(1)} %get-tuple-element.6.rows_in, f32[32,4,128]{2,1,0:T(4,128)S(1)} %get-tuple-element.7.best_in), custom_call_target="tpu_custom_call" | custom-call | tf_op jit(solution)/shard_map/deliver/pallas_call | solution.py:492

commit v7 on v6

--- a/solution.py
+++ b/solution.py
@@ -20,6 +20,7 @@
 RING = (1, 3, 2)
 FAR_FIRST = (2, 1, 3)
 EARLY = 12
+PIECES = 4
 
 
 def inverse_norm(values):
@@ -34,9 +35,9 @@
 
 def kernel(
     db_hbm, nb_hbm, vc_hbm, q_ref, aug_ref, best_ref,
-    q_v, q_t, db_ref, nb_ref, vc_ref, pool, mask_ref, wanted, total, coded, coded_in, ranges, ranges_in, ranges_of,
+    q_v, q_t, db_ref, nb_ref, vc_ref, pool, mask_ref, wanted, total, coded, coded_in, row_range, ranges, ranges_in, ranges_of,
     everyone, first_top, tops, y_in, y_best, z_in, late_in, bases,
-    q_sem, l_sem, a_recv, b_recv, c_recv, p_send, p_recv, g_recv, s_recv, ab_send, c_send,
+    q_sem, l_sem, a_recv, b_recv, c_recv, p_recv, g_recv, s_recv, ab_send, c_send, p_send,
     r_send, r_recv, g_send, s_send, y_send, y_recv, z_send, z_recv, t_send, t_recv, f_send, f_recv,
 ):
     rows_dev, features = db_ref.shape
@@ -238,32 +239,44 @@
 
     lax.fori_loop(0, 8, step_over, 0)
 
-    partial = total[...]
-    largest = jnp.max(jnp.abs(partial), axis=-1, keepdims=True)
-    largest = jnp.maximum(largest, 1e-30)
-    coded[...] = jnp.round(partial * (32760.0 / largest)).astype(jnp.int32).astype(jnp.int16)
-    spread_range = jnp.broadcast_to(largest * (1.0 / 32760.0), (rows_dev, 128))
-    ranges[...] = spread_range.T[0:8, :]
-
-    def quarter(dx, h):
-        start = (x + SIDE + dx) % SIDE * own_rows + h * half
-        return pl.ds(pl.multiple_of(start, half), half)
+    pieces = coded_in.shape[0]
+    piece_rows = own_rows // pieces
+
+    def quarter(dx, n, rows):
+        start = (x + SIDE + dx) % SIDE * own_rows + n * rows
+        return pl.ds(pl.multiple_of(start, rows), rows)
 
     def copy_r(dx):
         return remote(ranges, ranges_in.at[dx - 1], r_send, r_recv, across(dx))
 
-    def copy_p(dx, h):
-        return remote(
-            coded.at[quarter(dx, h)], coded_in.at[h, dx - 1], p_send.at[h], p_recv.at[h], across(dx)
+    def copy_p(dx, n):
+        return remote(
+            coded.at[quarter(dx, n, piece_rows)], coded_in.at[n, dx - 1], p_send, p_recv.at[n],
+            across(dx),
         )
 
     def sent(ref, sem):
         remote(ref, ref, sem, sem, sibling).wait_send()
 
-    for dx in FAR_FIRST:
-        copy_p(dx, 0).start()
+    for n in range(pieces):
+        for q in range(SIDE):
+            rows = pl.ds(q * own_rows + n * piece_rows, piece_rows)
+            partial = total[rows, :]
+            largest = jnp.max(jnp.abs(partial), axis=-1, keepdims=True)
+            largest = jnp.maximum(largest, 1e-30)
+            scaled = jnp.round(partial * (32760.0 / largest))
+            coded[rows, :] = scaled.astype(jnp.int32).astype(jnp.int16)
+            row_range[rows, :] = jnp.broadcast_to(largest * (1.0 / 32760.0), (piece_rows, 128))
+        if n == 0:
+            for dx in FAR_FIRST:
+                copy_p(dx, n).start()
+    ranges[...] = row_range[...].T[0:8, :]
     for dx in FAR_FIRST:
         copy_r(dx).start()
+    for n in range(1, pieces):
+        for dx in FAR_FIRST:
+            copy_p(dx, n).start()
+
     for load in query_loads:
         load.wait()
     panel_rows = 512
@@ -275,19 +288,17 @@
         return 0
 
     turns = queries_here // (4 * panel_rows)
-    lax.fori_loop(0, turns // 2, turn, 0)
-    sent(coded_in.at[0], p_send.at[0])
-    for dx in FAR_FIRST:
-        copy_p(dx, 1).start()
-    lax.fori_loop(turns // 2, turns, turn, 0)
+    lax.fori_loop(0, turns, turn, 0)
 
     others = (SIDE - 1) * half
     starts = (0, 2 * own_rows, 2 * own_rows + 2 * others)
     sizes = (own_rows, others, others)
 
-    def copy_g(i, h):
-        return remote(
-            everyone.at[pl.ds(h * half, half)], everyone.at[pl.ds(starts[1 + h] + i * half, half)],
+    def copy_g(i, n):
+        h, start = n * piece_rows // half, n * piece_rows % half
+        return remote(
+            everyone.at[pl.ds(n * piece_rows, piece_rows)],
+            everyone.at[pl.ds(starts[1 + h] + i * half + start, piece_rows)],
             g_send, g_recv.at[h], across(FAR_FIRST[i]),
         )
 
@@ -298,24 +309,26 @@
         )
 
     sums = []
-    for h in range(2):
-        kept = db_ref[quarter(0, h), :].astype(jnp.float32)
-        sums.append(kept * inverse_norm(kept) + total[quarter(0, h), :])
+    for n in range(pieces):
+        rows = quarter(0, n, piece_rows)
+        kept = db_ref[rows, :].astype(jnp.float32)
+        sums.append(kept * inverse_norm(kept) + total[rows, :])
     remote(ranges_in, ranges_in, r_send, r_recv, sibling).wait_recv()
     for dx in FAR_FIRST:
         across_range = jnp.broadcast_to(ranges_in[dx - 1, 0:1, :], (128, rows_dev))
         ranges_of[dx - 1] = across_range.T
 
-    for h in range(2):
-        summed = sums[h]
-        here = coded_in.at[h]
-        remote(here, here, p_send.at[h], p_recv.at[h], sibling).wait_recv()
+    for n in range(pieces):
+        summed = sums[n]
+        here = coded_in.at[n]
+        remote(here, here, p_send, p_recv.at[n], sibling).wait_recv()
         for dx in FAR_FIRST:
-            part = coded_in[h, dx - 1].astype(jnp.float32)
-            summed = summed + part * ranges_of[dx - 1, quarter(0, h), 0:1]
-        everyone[pl.ds(h * half, half), :] = (summed * inverse_norm(summed)).astype(jnp.bfloat16)
+            part = coded_in[n, dx - 1].astype(jnp.float32)
+            summed = summed + part * ranges_of[dx - 1, quarter(0, n, piece_rows), 0:1]
+        rows = pl.ds(n * piece_rows, piece_rows)
+        everyone[rows, :] = (summed * inverse_norm(summed)).astype(jnp.bfloat16)
         for i in range(SIDE - 1):
-            copy_g(i, h).start()
+            copy_g(i, n).start()
     copy_s(0).start()
 
     def hand_over(h):
@@ -401,7 +414,7 @@
     for h in range(2):
         for i in range(SIDE - 1):
             start = starts[1 + h] + i * half
-            aug_ref[quarter(-FAR_FIRST[i], h), :] = everyone[pl.ds(start, half), :]
+            aug_ref[quarter(-FAR_FIRST[i], h, half), :] = everyone[pl.ds(start, half), :]
 
     arrived(late_in, t_recv)
     best = tops[late_shares]
@@ -423,7 +436,7 @@
     sent(pool.at[pl.ds(0, 2 * (CHIPS - 1) * half)], ab_send)
     sent(pool.at[pl.ds(0, parity_rows)], c_send)
     sent(ranges_in, r_send)
-    sent(coded_in.at[1], p_send.at[1])
+    sent(coded_in, p_send)
     sent(everyone.at[pl.ds(0, 6 * half)], g_send)
     sent(everyone.at[pl.ds(0, 8 * half)], s_send)
     sent(y_in, y_send)
@@ -466,7 +479,8 @@
             pltpu.VMEM((fanout, rows_dev), jnp.int32),
             pltpu.VMEM((rows_dev, features), jnp.float32),
             pltpu.VMEM((rows_dev, features), jnp.int16),
-            pltpu.VMEM((2, SIDE - 1, own_rows // 2, features), jnp.int16),
+            pltpu.VMEM((PIECES, SIDE - 1, own_rows // PIECES, features), jnp.int16),
+            pltpu.VMEM((rows_dev, 128), jnp.float32),
             pltpu.VMEM((8, rows_dev), jnp.float32),
             pltpu.VMEM((SIDE - 1, 8, rows_dev), jnp.float32),
             pltpu.VMEM((SIDE - 1, rows_dev, 128), jnp.float32),
@@ -482,8 +496,8 @@
             dma((4,)),
         ]
         + [dma((CHIPS,))] * 2
-        + [dma((4,)), dma((2,)), dma((2,)), dma((2,)), dma((3,))]
-        + [dma] * 14,
+        + [dma((4,)), dma((PIECES,)), dma((2,)), dma((3,))]
+        + [dma] * 15,
         compiler_params=pltpu.CompilerParams(
             collective_id=0, has_side_effects=True, vmem_limit_bytes=56 * 2**20
         ),

time: 49.3 us -> 48.7 us (0.988)
  Pallas kernels: 48.5 us -> 47.9 us
    pallas_call x1, Pallas kernels: 47.7 us -> 47.1 us  [local(): pl.pallas_call(kernel, out_shape=(pltpu.VMEM((rows_dev, features), jnp.bf...]
where the time goes in v7:
time: 48.7 us; the launch traced here: 48.5 us
  Pallas kernels  47.9 us (98%)
  between operations  0.64 us (1%)
    pallas_call x1, Pallas kernels, local(): pl.pallas_call(kernel, out_shape=(pltpu.VMEM((rows_dev, features), jnp.bf...  47.1 us

profile of v7, /device:TPU:1, one launch (start us, length us, event | category | flops | bytes accessed | tf_op | source)
XLA Modules:
  0.0 48.5 jit_solution(10414376557556474422)
XLA Ops:
  0.6 47.1 %expand_and_score.1 = (bf16[256,768]{1,0:T(8,128)(2,1)S(1)}, f32[32,4,128]{2,1,0:T(4,128)S(1)}) custom-call(bf16[256,768]{1,0:T(8,128)(2,1)} %db_hbm.1, s32[16,256]{1,0:T(8,128)} %bitcast.3, s32[1,256]{1,0:T(1,128)} %bitcast.4, bf16[16384,768]{1,0:T(8,128)(2,1)} %q_ref.1), custom_call_target="tpu_custom_call" | custom-call | tf_op jit(solution)/shard_map/expand_and_score/pallas_call | solution.py:463
  47.8 0.8 %deliver.1 = (bf16[256,768]{1,0:T(8,128)(2,1)}, f32[32,4,128]{2,1,0:T(4,128)}) custom-call(bf16[256,768]{1,0:T(8,128)(2,1)S(1)} %get-tuple-element.6.rows_in, f32[32,4,128]{2,1,0:T(4,128)S(1)} %get-tuple-element.7.best_in), custom_call_target="tpu_custom_call" | custom-call | tf_op jit(solution)/shard_map/deliver/pallas_call | solution.py:506

commit v8 on v7

--- a/solution.py
+++ b/solution.py
@@ -20,6 +20,7 @@
 RING = (1, 3, 2)
 FAR_FIRST = (2, 1, 3)
 EARLY = 12
+MASKS_FIRST = 4
 PIECES = 4
 
 
@@ -36,7 +37,7 @@
 def kernel(
     db_hbm, nb_hbm, vc_hbm, q_ref, aug_ref, best_ref,
     q_v, q_t, db_ref, nb_ref, vc_ref, pool, mask_ref, wanted, total, coded, coded_in, row_range, ranges, ranges_in, ranges_of,
-    everyone, first_top, tops, y_in, y_best, z_in, late_in, bases,
+    own_scale, everyone, first_top, tops, y_in, y_best, z_in, late_in, bases,
     q_sem, l_sem, a_recv, b_recv, c_recv, p_recv, g_recv, s_recv, ab_send, c_send, p_send,
     r_send, r_recv, g_send, s_send, y_send, y_recv, z_send, z_recv, t_send, t_recv, f_send, f_recv,
 ):
@@ -151,23 +152,24 @@
             counts = []
             for v in range(2):
                 base = bases[part * 4 + u * 2 + v]
-                number = base + lax.broadcasted_iota(jnp.int32, (own_rows, rows_dev), 0)
-                count = jnp.zeros((own_rows, rows_dev), jnp.float32)
+                number = (base + lax.broadcasted_iota(jnp.int32, (own_rows, rows_dev), 0)).astype(jnp.int16)
+                count = jnp.zeros((own_rows, rows_dev), jnp.int16)
                 for k in range(fanout):
-                    count = count + jnp.where(wanted[pl.ds(k, 1), :] == number, 1.0, 0.0)
-                counts.append(count)
+                    here = jnp.broadcast_to(wanted[pl.ds(k, 1), :], (16, rows_dev)).astype(jnp.int16)
+                    here = jnp.concatenate([here] * (own_rows // 16), axis=0)
+                    count = count + jnp.where(here == number, jnp.int16(1), jnp.int16(0))
+                counts.append(count.astype(jnp.int32).astype(jnp.float32))
             both = jnp.concatenate(counts, axis=0)
             mask_ref[part, :, pl.ds(u * 2 * own_rows, 2 * own_rows)] = both.T.astype(jnp.bfloat16)
 
-    def first_masks(i, _):
-        build_mask(4 * i)
+    def mask_step(i, _):
+        build_mask(jnp.where(i < 2, 4 * i, i - 1 + (i - 2) // 3))
         return 0
 
-    def other_masks(i, _):
-        build_mask(i + 1 + i // 3)
-        return 0
-
-    lax.fori_loop(0, 2, first_masks, 0)
+    total[...] = jnp.zeros_like(total)
+    own_scale[...] = inverse_norm(db_ref[...].astype(jnp.float32))
+    groups = 8
+    lax.fori_loop(0, MASKS_FIRST, mask_step, 0)
 
     for step in RING:
         copy_a(0, step).wait_recv()
@@ -177,22 +179,25 @@
         for far in RING:
             copy_b(step, far).start()
 
-    lax.fori_loop(0, 6, other_masks, 0)
+    lax.fori_loop(MASKS_FIRST, groups, mask_step, 0)
 
     for step in RING:
         copy_b(0, step).wait_recv()
-        copy_c(SLOT_AT[(0, step)]).start()
         copy_a(step, 0).wait_recv()
-        copy_c(SLOT_AT[(step, 0)]).start()
+    remote(
+        block(1, 0, 0, 3 * own_rows), block(1, 1, 0, 3 * own_rows), c_send, c_recv.at[0], sibling
+    ).start()
+    remote(
+        block(4, 0, 0, 3 * own_rows), block(4, 1, 0, 3 * own_rows), c_send, c_recv.at[1], sibling
+    ).start()
 
     def pass_on(place):
         here = block(place, 0, 0, own_rows)
         remote(here, here, ab_send, a_recv.at[place], sibling).wait_recv()
         copy_c(place).start()
 
-    total[...] = jnp.zeros_like(total)
     own = db_ref[...]
-    own_inverse = inverse_norm(own.astype(jnp.float32))
+    own_inverse = own_scale[...]
 
     def take(g):
         rows = pool[pl.ds(pl.multiple_of(g * span, span), span), :]
@@ -484,6 +489,7 @@
             pltpu.VMEM((8, rows_dev), jnp.float32),
             pltpu.VMEM((SIDE - 1, 8, rows_dev), jnp.float32),
             pltpu.VMEM((SIDE - 1, rows_dev, 128), jnp.float32),
+            pltpu.VMEM((rows_dev, 1), jnp.float32),
             pltpu.VMEM((CORES * rows_dev, features), jnp.bfloat16),
             pltpu.VMEM((CHIPS, 8, share), jnp.float32),
             pltpu.VMEM((CHIPS, share // 128, 128), jnp.float32),

time: 48.7 us -> 48.4 us (level)
  no operation moved by 1% of the time
where the time goes in v8:
time: 48.4 us; the launch traced here: 48.3 us
  Pallas kernels  47.7 us (99%)
  between operations  0.64 us (1%)
    pallas_call x1, Pallas kernels, local(): pl.pallas_call(kernel, out_shape=(pltpu.VMEM((rows_dev, features), jnp.bf...  46.9 us

profile of v8, /device:TPU:1, one launch (start us, length us, event | category | flops | bytes accessed | tf_op | source)
XLA Modules:
  0.0 48.3 jit_solution(12860872376454126105)
XLA Ops:
  0.6 46.9 %expand_and_score.1 = (bf16[256,768]{1,0:T(8,128)(2,1)S(1)}, f32[32,4,128]{2,1,0:T(4,128)S(1)}) custom-call(bf16[256,768]{1,0:T(8,128)(2,1)} %db_hbm.1, s32[16,256]{1,0:T(8,128)} %bitcast.3, s32[1,256]{1,0:T(1,128)} %bitcast.4, bf16[16384,768]{1,0:T(8,128)(2,1)} %q_ref.1), custom_call_target="tpu_custom_call" | custom-call | tf_op jit(solution)/shard_map/expand_and_score/pallas_call | solution.py:468
  47.5 0.8 %deliver.1 = (bf16[256,768]{1,0:T(8,128)(2,1)}, f32[32,4,128]{2,1,0:T(4,128)}) custom-call(bf16[256,768]{1,0:T(8,128)(2,1)S(1)} %get-tuple-element.6.rows_in, f32[32,4,128]{2,1,0:T(4,128)S(1)} %get-tuple-element.7.best_in), custom_call_target="tpu_custom_call" | custom-call | tf_op jit(solution)/shard_map/deliver/pallas_call | solution.py:512

commit v9 on v8

--- a/solution.py
+++ b/solution.py
@@ -120,10 +120,10 @@
     for step in RING:
         copy_a(0, step).start()
         copy_b(step, 0).start()
-    copy_c(0).start()
     for step in RING:
         copy_a(step, 0).start()
         copy_b(0, step).start()
+    copy_c(0).start()
 
     queries_here = q_v.shape[0]
     piece = queries_here // 4
@@ -229,10 +229,11 @@
             for u in range(4):
                 here = block(part * 4 + u, 0, 0, own_rows)
                 remote(here, here, ab_send, a_recv.at[part * 4 + u], sibling).wait_recv()
-            remote(
-                block(part * 4, 0, 0, span), block(part * 4, 1, 0, span), c_send,
-                c_recv.at[part], sibling,
-            ).start()
+                if u % 2:
+                    remote(
+                        block(part * 4 + u - 1, 0, 0, span // 2),
+                        block(part * 4 + u - 1, 1, 0, span // 2), c_send, c_recv.at[part], sibling,
+                    ).start()
 
         @pl.when(part >= 4)
         def _():

time: 48.4 us -> 48.3 us (level)
  no operation moved by 1% of the time
where the time goes in v9:
time: 48.3 us; the launch traced here: 48.1 us
  Pallas kernels  47.5 us (98%)
  between operations  0.64 us (1%)
    pallas_call x1, Pallas kernels, local(): pl.pallas_call(kernel, out_shape=(pltpu.VMEM((rows_dev, features), jnp.bf...  46.7 us

profile of v9, /device:TPU:1, one launch (start us, length us, event | category | flops | bytes accessed | tf_op | source)
XLA Modules:
  0.0 48.1 jit_solution(15514392383156540684)
XLA Ops:
  0.6 46.7 %expand_and_score.1 = (bf16[256,768]{1,0:T(8,128)(2,1)S(1)}, f32[32,4,128]{2,1,0:T(4,128)S(1)}) custom-call(bf16[256,768]{1,0:T(8,128)(2,1)} %db_hbm.1, s32[16,256]{1,0:T(8,128)} %bitcast.3, s32[1,256]{1,0:T(1,128)} %bitcast.4, bf16[16384,768]{1,0:T(8,128)(2,1)} %q_ref.1), custom_call_target="tpu_custom_call" | custom-call | tf_op jit(solution)/shard_map/expand_and_score/pallas_call | solution.py:469
  47.3 0.8 %deliver.1 = (bf16[256,768]{1,0:T(8,128)(2,1)}, f32[32,4,128]{2,1,0:T(4,128)}) custom-call(bf16[256,768]{1,0:T(8,128)(2,1)S(1)} %get-tuple-element.6.rows_in, f32[32,4,128]{2,1,0:T(4,128)S(1)} %get-tuple-element.7.best_in), custom_call_target="tpu_custom_call" | custom-call | tf_op jit(solution)/shard_map/deliver/pallas_call | solution.py:513

commit v10 on v9

--- a/solution.py
+++ b/solution.py
@@ -388,7 +388,7 @@
 
     copy_s(0).wait_recv()
     for k in range(shares):
-        if k == shares * 3 // 4:
+        if k == shares // 2:
             hand_over(0)
         first_top[k] = folded_scores(first, second, k)
     copy_s(1).wait_recv()

time: 48.3 us -> 48.3 us (level)
  no operation moved by 1% of the time
where the time goes in v10:
time: 48.3 us; the launch traced here: 48.1 us
  Pallas kernels  47.5 us (98%)
  between operations  0.64 us (1%)
    pallas_call x1, Pallas kernels, local(): pl.pallas_call(kernel, out_shape=(pltpu.VMEM((rows_dev, features), jnp.bf...  46.7 us

profile of v10, /device:TPU:1, one launch (start us, length us, event | category | flops | bytes accessed | tf_op | source)
XLA Modules:
  0.0 48.1 jit_solution(1161937440051811306)
XLA Ops:
  0.6 46.7 %expand_and_score.1 = (bf16[256,768]{1,0:T(8,128)(2,1)S(1)}, f32[32,4,128]{2,1,0:T(4,128)S(1)}) custom-call(bf16[256,768]{1,0:T(8,128)(2,1)} %db_hbm.1, s32[16,256]{1,0:T(8,128)} %bitcast.3, s32[1,256]{1,0:T(1,128)} %bitcast.4, bf16[16384,768]{1,0:T(8,128)(2,1)} %q_ref.1), custom_call_target="tpu_custom_call" | custom-call | tf_op jit(solution)/shard_map/expand_and_score/pallas_call | solution.py:469
  47.3 0.8 %deliver.1 = (bf16[256,768]{1,0:T(8,128)(2,1)}, f32[32,4,128]{2,1,0:T(4,128)}) custom-call(bf16[256,768]{1,0:T(8,128)(2,1)S(1)} %get-tuple-element.6.rows_in, f32[32,4,128]{2,1,0:T(4,128)S(1)} %get-tuple-element.7.best_in), custom_call_target="tpu_custom_call" | custom-call | tf_op jit(solution)/shard_map/deliver/pallas_call | solution.py:513
